TPU v7x, 512 devices: a whole 4x4x16 slice. The times are simulated.
512 devices in a mesh: gx: 64 (over z, x_hi, core), gy: 8 (over y, x_lo).
Axes of the slice: x: 4 (x_hi: 2, x_lo: 2; x = x_hi * 2 + x_lo), y: 4, z: 16, core: 2. Of those that a mesh axis runs over, the one named last changes fastest.
Arguments:
- tokens: bfloat16 [512, 8192], P('gx', 'gy'), may hold values from -6 to 6
- out_grad: bfloat16 [512, 8192], P('gx', 'gy'), may hold values from -6 to 6
- gate_weight: bfloat16 [8192, 16384], P('gy', 'gx'), may hold values from -0.0625 to 0.0625
- up_weight: bfloat16 [8192, 16384], P('gy', 'gx'), may hold values from -0.0625 to 0.0625
- down_weight: bfloat16 [16384, 8192], P('gx', 'gy'), may hold values from -0.046875 to 0.046875
Outputs:
- input_grad: bfloat16 [512, 8192], P('gx', 'gy')
- gate_grad: bfloat16 [8192, 16384], P('gy', 'gx')
- up_grad: bfloat16 [8192, 16384], P('gy', 'gx')
- down_grad: bfloat16 [16384, 8192], P('gx', 'gy')
All inputs are finite; a program needn't handle non-finite values.
Results may differ from a plain program's by a relative error of at most 0.0049.
Values may be sent and summed in bfloat16 or wider, within the bound.
A program may use at most 64 MiB of HBM per device.

v0:
```python
import jax
import jax.numpy as jnp
from jax import lax
from jax.sharding import PartitionSpec as P


def pointwise(gate, up, hidden_grad):
    sigma = jax.nn.sigmoid(gate)
    active = gate * sigma
    hidden = (active * up).astype(jnp.bfloat16)
    dgate = (hidden_grad * up * sigma * (1.0 + gate * (1.0 - sigma))).astype(jnp.bfloat16)
    dup = (hidden_grad * active).astype(jnp.bfloat16)
    return (hidden, dgate, dup)


def contract_rows(left, right):
    return lax.dot_general(
        left, right, (((0,), (0,)), ((), ())), preferred_element_type=jnp.float32
    )


def contract_cols(left, right):
    return lax.dot_general(
        left, right, (((1,), (1,)), ((), ())), preferred_element_type=jnp.float32
    )


def per_device(tokens, out_grad, gate_weight, up_weight, down_weight):
    all_tokens, all_grads = (
        lax.all_gather(tokens, "gx", axis=0, tiled=True),
        lax.all_gather(out_grad, "gx", axis=0, tiled=True),
    )
    gate_part = jnp.dot(all_tokens, gate_weight, preferred_element_type=jnp.float32)
    up_part = jnp.dot(all_tokens, up_weight, preferred_element_type=jnp.float32)
    grad_part = contract_cols(all_grads, down_weight)
    gate, up, hidden_grad = lax.psum((gate_part, up_part, grad_part), "gy")
    hidden, dgate, dup = pointwise(gate, up, hidden_grad)
    input_grad = lax.psum_scatter(
        contract_cols(dgate, gate_weight) + contract_cols(dup, up_weight),
        "gx",
        scatter_dimension=0,
        tiled=True,
    )
    factor = 1.0 / jnp.sqrt(jnp.float32(all_tokens.shape[0]))
    down_grad = (contract_rows(hidden, all_grads) * factor).astype(jnp.bfloat16)
    gate_grad = (contract_rows(all_tokens, dgate) * factor).astype(jnp.bfloat16)
    up_grad = (contract_rows(all_tokens, dup) * factor).astype(jnp.bfloat16)
    return (input_grad.astype(jnp.bfloat16), gate_grad, up_grad, down_grad)


def solution(mesh):
    return jax.shard_map(
        per_device,
        mesh=mesh,
        in_specs=(P("gx", "gy"), P("gx", "gy"), P("gy", "gx"), P("gy", "gx"), P("gx", "gy")),
        out_specs=(P("gx", "gy"), P("gy", "gx"), P("gy", "gx"), P("gx", "gy")),
        check_vma=False,
    )
```

profile of v0, /device:TPU:1, one launch (start us, length us, event | category | flops | bytes accessed | tf_op | source)
XLA Modules:
  0.0 612.4 jit_solution(10351450743724018121)
XLA Ops:
  7.2 0.0 copy-start
  7.2 0.0 copy-start.2
  7.2 0.0 all-gather.5.cloned.1.call-start
  7.2 0.7 all-gather.5.cloned.1.call-update
  7.9 0.0 all-gather.3.cloned.1.call-start
  8.0 0.7 all-gather.3.cloned.1.call-update
  8.7 0.0 copy-start.4
  8.7 0.0 all-reduce.3.cloned.1.call-start
  8.7 148.0 %all-gather.5.cloned.1.call-done = bf16[512,1024]{1,0:T(8,128)(2,1)} async-done(((bf16[8,1024]{1,0:T(8,128)(2,1)}), bf16[512,1024]{1,0:T(8,128)(2,1)}) %all-gather.5.cloned.1.call-update) | async-done | bytes 1048592 | tf_op jit(solution)/shard_map/all_gather | solution.py:30
  156.8 0.0 copy-done
  156.8 0.0 copy-start.1
  156.8 2.5 fusion.10
  159.3 0.0 copy-done.2
  159.3 0.0 copy-done.1
  159.3 1.2 fusion.9
  160.6 134.8 %all-gather.3.cloned.1.call-done = bf16[512,1024]{1,0:T(8,128)(2,1)} async-done(((bf16[8,1024]{1,0:T(8,128)(2,1)}), bf16[512,1024]{1,0:T(8,128)(2,1)}) %all-gather.3.cloned.1.call-update) | async-done | bytes 1048592 | tf_op jit(solution)/shard_map/all_gather | solution.py:31
  295.3 0.0 copy-done.4
  295.3 2.5 fusion.8
  297.8 0.0 all-reduce.3.cloned.1.call-update
  297.9 0.0 reduce-scatter.2.cloned.1.call-start
  297.9 99.2 %all-reduce.3.cloned.1.call-done = (f32[512,256]{1,0:T(8,128)}, f32[512,256]{1,0:T(8,128)}, f32[512,256]{1,0:T(8,128)}) async-done(((f32[512,256]{1,0:T(8,128)}, f32[512,256]{1,0:T(8,128)}, f32[512,256]{1,0:T(8,128)}), (f32[512,256]{1,0:T(8,128)}, f32[512,256]{1,0:T(8,128)}, f32[512,256]{1,0:T(8,128)})) %all-reduce.3.cloned.1.call-update) | async-done | bytes 1572880 | tf_op jit(solution)/shard_map/psum | solution.py:36
  397.1 1.6 multiply_convert_fusion.1
  398.7 0.5 fusion.11
  399.2 1.8 convolution_add_fusion
  401.0 0.0 reduce-scatter.2.cloned.1.call-update
  401.0 0.5 fusion.4
  401.5 0.0 copy-start.3
  401.5 1.0 copy.9
  402.5 0.5 fusion.3
  402.9 1.0 copy.10
  403.9 0.0 copy-done.3
  403.9 2.5 fusion.2
  406.4 198.0 %reduce-scatter.2.cloned.1.call-done = f32[8,1024]{1,0:T(8,128)} async-done(((f32[512,1024]{1,0:T(8,128)}), f32[8,1024]{1,0:T(8,128)}) %reduce-scatter.2.cloned.1.call-update) | async-done | bytes 32784 | tf_op jit(solution)/shard_map/reduce_scatter | solution.py:38
  604.5 1.4 convert_element_type.29
Async XLA Ops:
  7.2 149.6 %copy-start = (bf16[1024,256]{1,0:T(8,128)(2,1)S(1)}, bf16[1024,256]{1,0:T(8,128)(2,1)}, u32[]{:S(2)}) copy-start(bf16[1024,256]{1,0:T(8,128)(2,1)} %param.7) | copy-start | bytes 1572868
  7.2 152.1 %copy-start.2 = (bf16[1024,256]{1,0:T(8,128)(2,1)S(1)}, bf16[1024,256]{1,0:T(8,128)(2,1)}, u32[]{:S(2)}) copy-start(bf16[1024,256]{1,0:T(8,128)(2,1)} %param.8) | copy-start | bytes 1572868
  7.2 149.6 %all-gather.5.cloned.1.call-start = ((), (), s32[]{:S(2)}) async-start(), calls=%async_computation.2 | async-start | bytes 1064960 | tf_op jit(solution)/shard_map/all_gather | solution.py:30
  7.9 287.4 %all-gather.3.cloned.1.call-start = ((), (), s32[]{:S(2)}) async-start(), calls=%async_computation.1 | async-start | bytes 1064960 | tf_op jit(solution)/shard_map/all_gather | solution.py:31
  8.7 286.7 %copy-start.4 = (bf16[256,1024]{1,0:T(8,128)(2,1)S(1)}, bf16[256,1024]{1,0:T(8,128)(2,1)}, u32[]{:S(2)}) copy-start(bf16[256,1024]{1,0:T(8,128)(2,1)} %param.9) | copy-start | bytes 1572868
  8.7 388.4 %all-reduce.3.cloned.1.call-start = ((), (), s32[]{:S(2)}) async-start(), calls=%async_computation.4 | async-start | bytes 3145728 | tf_op jit(solution)/shard_map/psum | solution.py:36
  156.8 2.6 copy-start.1
  297.9 306.6 %reduce-scatter.2.cloned.1.call-start = ((), (), s32[]{:S(2)}) async-start(), calls=%async_computation.3 | async-start | bytes 2129920 | tf_op jit(solution)/shard_map/reduce_scatter | solution.py:38
  401.5 2.5 copy-start.3
Sparse Core Ops, SparseCore 0:
  11.3 145.4 all-gather.4
  160.1 135.2 all-gather.2
  299.1 97.9 all-reduce.2
  401.6 202.8 reduce-scatter.1
where the time goes:
time: 623 us; the launch traced here: 612 us
  waiting for transfers between devices  581 us (93%)
  between operations  13.8 us (2%)
  matrix products  12 us (2%)
    reduce_scatter x1, waiting for transfers between devices, per_device(): lax.psum_scatter(contract_cols(dgate, gate_weight) + contract_cols(dup, u...  198 us
    all_gather x1, waiting for transfers between devices, per_device(): lax.all_gather(tokens, 'gx', axis=0, tiled=True)  148 us
    all_gather x1, waiting for transfers between devices, per_device(): lax.all_gather(out_grad, 'gx', axis=0, tiled=True)  135 us
    psum x1, waiting for transfers between devices, per_device(): gate, up, hidden_grad = lax.psum((gate_part, up_part, grad_part), 'gy')  99.2 us
  transfers between devices with their start and end apart: 4, of which 4 were waited for; matrix products, arithmetic and copies ran while one was open for 1% of the time, Pallas kernels for 0%

commit v1 on v0

v1 whole, which is shorter than its diff:
```python
import jax
import jax.numpy as jnp
from jax import lax
from jax.experimental import pallas as pl
from jax.experimental.pallas import tpu as pltpu
from jax.sharding import PartitionSpec as P

MESH = pl.DeviceIdType.MESH
BF16, F32 = jnp.bfloat16, jnp.float32

NEAR = (0, 1, -1, 2)
FAR_ORDER = (2, 1, 3)
NEAR_ORDER = (3, 1, 2)


def dot(a, b, dims):
    return lax.dot_general(a, b, (dims, ((), ())), preferred_element_type=F32)


def kernel(tok_ref, grad_ref, gw_hbm, uw_hbm, dw_hbm,
           ig_ref, gg_ref, ug_ref, dg_ref,
           gw, uw, dw, ex_out, ex_in, x, part, b_in, h, ig, core_in,
           near_out, near_own, near_in, far_out, far_in,
           w_sem, send_sem, recv_sem):
    gx, gy = lax.axis_index("gx"), lax.axis_index("gy")
    z, xh, c = gx // 4, (gx // 2) % 2, gx % 2
    y, xl = gy // 2, gy % 2

    def along(dz=0, other_x=False, other_core=False):
        zz = (z + dz + 16) % 16
        xx = 1 - xh if other_x else xh
        cc = 1 - c if other_core else c
        return (zz * 4 + xx * 2 + cc, gy)

    peers = [(dy, dx) for dy in (2, 1, 3, 0) for dx in (1, 0) if dy or dx]

    def across(dy, dx):
        return ((y + dy) % 4) * 2 + (xl + dx) % 2

    loads = [pltpu.make_async_copy(s, d, w_sem.at[i])
             for i, (s, d) in enumerate(((gw_hbm, gw), (uw_hbm, uw), (dw_hbm, dw)))]
    for cp in loads:
        cp.start()

    barrier = pltpu.get_barrier_semaphore()
    met = [along(dz) for dz in (8, 4, -4, 2, -2, 1, -1)]
    met += [along(dz, other_x=True) for dz in (8, 4, -4, 0)]
    met += [along(other_core=True)]
    met += [(gx, across(dy, dx)) for dy, dx in peers]
    for dev in met:
        pl.semaphore_signal(barrier, inc=1, device_id=dev, device_id_type=MESH)

    first = c == 0
    tok, grad = tok_ref[...].astype(F32), grad_ref[...].astype(F32)
    mine = jnp.where(first, tok, grad)
    ex_out[...] = jnp.where(first, grad, tok)
    pl.semaphore_wait(barrier, len(met))

    sent = []

    def push(src, dst, dev):
        k = len(sent)
        cp = pltpu.make_async_remote_copy(
            src_ref=src, dst_ref=dst, send_sem=send_sem.at[k], recv_sem=recv_sem.at[k],
            device_id=dev, device_id_type=MESH)
        cp.start()
        sent.append(cp)
        return cp

    sibling = along(other_core=True)
    partner = along(other_x=True)

    push(ex_out, ex_in, sibling).wait_recv()
    theirs = ex_in[...]
    block = jnp.concatenate(
        [jnp.where(first, mine, theirs), jnp.where(first, theirs, mine)], axis=0)
    x[c, 0, 0, 0] = block.astype(BF16)

    far = [push(x.at[c, 0, 0, 0], x.at[c, 0, 0, 4 - i], along(4 * i)) for i in FAR_ORDER]
    for cp in far:
        cp.wait_recv()
    near = [push(x.at[c, 0, 0], x.at[c, 0, n], along(-NEAR[n])) for n in NEAR_ORDER]
    to_x = [push(x.at[c, 0, 0], x.at[c, 1, 0], partner)]
    to_core = [push(x.at[c, 0, 0], x.at[c, 0, 0], sibling)]
    for n, cp in zip((1, 2, 3), (near[1], near[2], near[0])):
        cp.wait_recv()
        to_x.append(push(x.at[c, 0, n], x.at[c, 1, n], partner))
        to_core.append(push(x.at[c, 0, n], x.at[c, 0, n], sibling))

    def products(k):
        rows = x[0, k].reshape(256, 1024)
        part[k, :, :, 0:256] = dot(rows, gw[...], ((1,), (0,))).reshape(8, 32, 256)
        part[k, :, :, 256:512] = dot(rows, uw[...], ((1,), (0,))).reshape(8, 32, 256)
        part[k, :, :, 512:768] = dot(
            x[1, k].reshape(256, 1024), dw[...], ((1,), (1,))).reshape(8, 32, 256)
        return [push(part.at[k, across(dy, dx)], b_in.at[k, s], (gx, across(dy, dx)))
                for s, (dy, dx) in enumerate(peers)]

    def pointwise(k, arrived):
        for cp in arrived:
            cp.wait_recv()
        total = part[k, gy]
        for s in range(7):
            total = total + b_in[k, s]
        gate, up, hgrad = total[:, 0:256], total[:, 256:512], total[:, 512:768]
        sigma = jax.nn.sigmoid(gate)
        act = gate * sigma
        h[k, gy, :, 0:256] = (act * up).astype(BF16)
        h[k, gy, :, 256:512] = (hgrad * up * sigma * (1.0 + gate * (1.0 - sigma))).astype(BF16)
        h[k, gy, :, 512:768] = (hgrad * act).astype(BF16)
        return [push(h.at[k, gy], h.at[k, gy], (gx, across(dy, dx))) for dy, dx in peers]

    def input_products(k, arrived):
        for cp in arrived:
            cp.wait_recv()
        hh = h[k].reshape(256, 768)
        for j in range(2):
            cols = slice(512 * j, 512 * j + 512)
            v = dot(hh[:, 256:512], gw[cols, :], ((1,), (1,)))
            v = v + dot(hh[:, 512:768], uw[cols, :], ((1,), (1,)))
            ig[k, :, :, :, cols] = v.reshape(16, 2, 8, 512)
        return push(ig.at[k, :, 1 - c], core_in.at[k], sibling)

    def send_near(k, arrived):
        arrived.wait_recv()
        for n in range(4):
            for f in range(4):
                s = 4 * n + f
                v = ig[k, s, c] + core_in[k, s]
                v = jnp.concatenate([v[:, 0:512], v[:, 512:1024]], axis=0)
                if n == 0:
                    near_own[k, f] = v
                else:
                    near_out[k, n, f] = v.astype(BF16)
        return [push(near_out.at[k, n], near_in.at[k, n], along(NEAR[n])) for n in NEAR_ORDER]

    def send_far(k, arrived):
        for cp in arrived:
            cp.wait_recv()
        for f in range(4):
            v = near_own[k, f]
            for n in (1, 2, 3):
                v = v + near_in[k, n, f].astype(F32)
            if k == 0 and f == 0:
                near_own[k, f] = v
            else:
                far_out[k, f] = v.astype(BF16)
        order = FAR_ORDER if k == 0 else FAR_ORDER + (0,)
        return [push(far_out.at[k, f], far_in.at[k, f], along(4 * f, other_x=k == 1))
                for f in order]

    for cp in loads:
        cp.wait()
    for cp in to_core:
        cp.wait_recv()
    b0 = products(0)

    to_core = []
    for n in range(4):
        to_x[n].wait_recv()
        to_core.append(push(x.at[c, 1, n], x.at[c, 1, n], sibling))
    for cp in to_core:
        cp.wait_recv()
    b1 = products(1)

    c0 = pointwise(0, b0)
    c1 = pointwise(1, b1)
    i0 = input_products(0, c0)
    n0 = send_near(0, i0)
    i1 = input_products(1, c1)
    n1 = send_near(1, i1)
    f0 = send_far(0, n0)
    f1 = send_far(1, n1)

    factor = 1.0 / jnp.sqrt(F32(512))

    @pl.loop(0, 4)
    def _(i):
        cols = pl.ds(pl.multiple_of(i * 256, 256), 256)
        hh = h[...].reshape(512, 768)
        t = x[0, :, :, :, :, cols].reshape(512, 256)
        gg_ref[cols, :] = (dot(t, hh[:, 256:512], ((0,), (0,))) * factor).astype(BF16)
        ug_ref[cols, :] = (dot(t, hh[:, 512:768], ((0,), (0,))) * factor).astype(BF16)
        g = x[1, :, :, :, :, cols].reshape(512, 256)
        dg_ref[:, cols] = (dot(hh[:, 0:256], g, ((0,), (0,))) * factor).astype(BF16)

    for cp in f0 + f1:
        cp.wait_recv()
    v = near_own[0, 0] + far_in[1, 0].astype(F32)
    for f in (1, 2, 3):
        v = v + (far_in[0, f].astype(F32) + far_in[1, f].astype(F32))
    ig_ref[...] = jnp.concatenate([v[0:8], v[8:16]], axis=1).astype(BF16)

    for cp in sent:
        cp.wait_send()


COPIES = 62


def per_device(tokens, out_grad, gate_weight, up_weight, down_weight):
    vmem = pl.BlockSpec(memory_space=pltpu.VMEM)
    hbm = pl.BlockSpec(memory_space=pl.ANY)
    shape = jax.ShapeDtypeStruct
    return pl.pallas_call(
        kernel,
        out_shape=(shape((8, 1024), BF16), shape((1024, 256), BF16),
                   shape((1024, 256), BF16), shape((256, 1024), BF16)),
        in_specs=[vmem, vmem, hbm, hbm, hbm],
        out_specs=(vmem,) * 4,
        scratch_shapes=[
            pltpu.VMEM((1024, 256), BF16),
            pltpu.VMEM((1024, 256), BF16),
            pltpu.VMEM((256, 1024), BF16),
            pltpu.VMEM((8, 1024), F32),
            pltpu.VMEM((8, 1024), F32),
            pltpu.VMEM((2, 2, 4, 4, 16, 1024), BF16),
            pltpu.VMEM((2, 8, 32, 768), F32),
            pltpu.VMEM((2, 7, 32, 768), F32),
            pltpu.VMEM((2, 8, 32, 768), BF16),
            pltpu.VMEM((2, 16, 2, 8, 1024), F32),
            pltpu.VMEM((2, 16, 8, 1024), F32),
            pltpu.VMEM((2, 4, 4, 16, 512), BF16),
            pltpu.VMEM((2, 4, 16, 512), F32),
            pltpu.VMEM((2, 4, 4, 16, 512), BF16),
            pltpu.VMEM((2, 4, 16, 512), BF16),
            pltpu.VMEM((2, 4, 16, 512), BF16),
            pltpu.SemaphoreType.DMA((3,)),
            pltpu.SemaphoreType.DMA((COPIES,)),
            pltpu.SemaphoreType.DMA((COPIES,)),
        ],
        compiler_params=pltpu.CompilerParams(
            collective_id=0, has_side_effects=True, vmem_limit_bytes=48 << 20),
        cost_estimate=pl.CostEstimate(
            flops=2 * 8 * 512 * 1024 * 256, bytes_accessed=4 << 20, transcendentals=64 * 256),
    )(tokens, out_grad, gate_weight, up_weight, down_weight)


def solution(mesh):
    return jax.shard_map(
        per_device,
        mesh=mesh,
        in_specs=(P("gx", "gy"), P("gx", "gy"), P("gy", "gx"), P("gy", "gx"), P("gx", "gy")),
        out_specs=(P("gx", "gy"), P("gy", "gx"), P("gy", "gx"), P("gx", "gy")),
        check_vma=False,
    )
```

time: 623 us -> 103 us (0.17); the launches traced: 612 us -> 102 us
  waiting for transfers between devices: 581 us -> 0 us
  Pallas kernels: 0 us -> 94.1 us
  between operations: 13.8 us -> 0.65 us
  matrix products: 12 us -> 0 us
    all_gather x2 -> x0, waiting for transfers between devices: 283 us -> none  [the longest x1 148 us: per_device(): lax.all_gather(tokens, 'gx', axis=0, tiled=True)]
    reduce_scatter x1 -> x0, waiting for transfers between devices: 198 us -> none  [per_device(): lax.psum_scatter(contract_cols(dgate, gate_weight) + contract_cols(dup, u...]
    psum x1 -> x0, waiting for transfers between devices: 99.2 us -> none  [per_device(): gate, up, hidden_grad = lax.psum((gate_part, up_part, grad_part), 'gy')]
    pallas_call x0 -> x1, Pallas kernels: none -> 94.1 us  [per_device(): pl.pallas_call(kernel, out_shape=(shape((8, 1024), BF16), shape((1024, 25...]
    dot_general x8 -> x0, matrix products: 12 us -> none  [the longest x3 4.77 us: contract_cols(): lax.dot_general(left, right, (((1,), (1,)), ((), ())), preferred_element_...]
  transfers between devices with their start and end apart: 4 -> 0, of which waited for: 4 -> 0; matrix products, arithmetic and copies ran while one was open for 1% -> 0% of each run, Pallas kernels for 0% -> 0%
where the time goes in v1:
time: 103 us; the launch traced here: 102 us
  Pallas kernels  94.1 us (91%)
  local copies, waits for them, and re-layouts  7.54 us (7%)
    pallas_call x1, Pallas kernels, per_device(): pl.pallas_call(kernel, out_shape=(shape((8, 1024), BF16), shape((1024, 25...  94.1 us
    unnamed x14, local copies, waits for them, and re-layouts  7.54 us

profile of v1, /device:TPU:1, one launch (start us, length us, event | category | flops | bytes accessed | tf_op | source)
XLA Modules:
  0.0 102.2 jit_solution(2706551791503407629)
XLA Ops:
  0.6 0.0 copy-start
  0.6 1.0 %copy-done = bf16[1024,256]{1,0:T(8,128)(2,1)S(1)} copy-done((bf16[1024,256]{1,0:T(8,128)(2,1)S(1)}, bf16[1024,256]{1,0:T(8,128)(2,1)}, u32[]{:S(2)}) %copy-start) | copy-done | bytes 524312
  1.7 0.0 copy-start.1
  1.7 1.0 %copy-done.1 = bf16[1024,256]{1,0:T(8,128)(2,1)S(1)} copy-done((bf16[1024,256]{1,0:T(8,128)(2,1)S(1)}, bf16[1024,256]{1,0:T(8,128)(2,1)}, u32[]{:S(2)}) %copy-start.1) | copy-done | bytes 524312
  2.7 0.0 copy-start.2
  2.7 1.0 %copy-done.2 = bf16[256,1024]{1,0:T(8,128)(2,1)S(1)} copy-done((bf16[256,1024]{1,0:T(8,128)(2,1)S(1)}, bf16[256,1024]{1,0:T(8,128)(2,1)}, u32[]{:S(2)}) %copy-start.2) | copy-done | bytes 524312
  3.8 0.0 copy-start.3
  3.8 0.7 copy-done.3
  4.5 0.0 copy-start.4
  4.5 0.7 copy-done.4
  5.2 94.1 %shard_map.84 = (bf16[8,1024]{1,0:T(8,128)(2,1)S(1)}, bf16[1024,256]{1,0:T(8,128)(2,1)S(1)}, bf16[1024,256]{1,0:T(8,128)(2,1)S(1)}, bf16[256,1024]{1,0:T(8,128)(2,1)S(1)}) custom-call(bf16[8,1024]{1,0:T(8,128)(2,1)S(1)} %copy-done.3, bf16[8,1024]{1,0:T(8,128)(2,1)S(1)} %copy-done.4, bf16[1024,256]{1,0:T(8,128)(2,1)S(1)} %copy-done, ...), custom_call_target="tpu_custom_call" | custom-call | flops 2147483648 | bytes 4194304 | tf_op jit(solution)/shard_map/pallas_call | solution.py:205
  99.3 0.6 copy.13
  99.9 0.8 copy.14
  100.7 0.8 copy.15
  101.5 0.8 copy.16
Async XLA Ops:
  0.6 1.0 %copy-start = (bf16[1024,256]{1,0:T(8,128)(2,1)S(1)}, bf16[1024,256]{1,0:T(8,128)(2,1)}, u32[]{:S(2)}) copy-start(bf16[1024,256]{1,0:T(8,128)(2,1)} %gw_hbm.1) | copy-start | bytes 1572868
  1.7 1.0 %copy-start.1 = (bf16[1024,256]{1,0:T(8,128)(2,1)S(1)}, bf16[1024,256]{1,0:T(8,128)(2,1)}, u32[]{:S(2)}) copy-start(bf16[1024,256]{1,0:T(8,128)(2,1)} %uw_hbm.1) | copy-start | bytes 1572868
  2.7 1.0 %copy-start.2 = (bf16[256,1024]{1,0:T(8,128)(2,1)S(1)}, bf16[256,1024]{1,0:T(8,128)(2,1)}, u32[]{:S(2)}) copy-start(bf16[256,1024]{1,0:T(8,128)(2,1)} %dw_hbm.1) | copy-start | bytes 1572868
  3.8 0.7 copy-start.3
  4.5 0.7 copy-start.4

commit v2 on v1

v2 whole, which is shorter than its diff:
```python
import jax
import jax.numpy as jnp
from jax import lax
from jax.experimental import pallas as pl
from jax.experimental.pallas import tpu as pltpu
from jax.sharding import PartitionSpec as P

MESH = pl.DeviceIdType.MESH
BF16, F32 = jnp.bfloat16, jnp.float32

NEAR = (0, 1, -1, 2)
FAR_ORDER = (2, 1, 3)
CHUNKS = range(4)
COPIES = 96


def dot(a, b, dims):
    return lax.dot_general(a, b, (dims, ((), ())), preferred_element_type=F32)


def kernel(tok_hbm, grad_hbm, gw_hbm, uw_hbm, dw_hbm,
           ig_hbm, gg_hbm, ug_hbm, dg_hbm,
           tok_v, grad_v, gw, uw, dw, ex_out, ex_in, x, part, b_relay, b_sum, b_in, h,
           ig, core_in, near_out, near_own, near_in, far_out, far_in,
           ig_v, gg_v, ug_v, dg_v,
           load_sem, store_sem, send_sem, recv_sem):
    gx, gy = lax.axis_index("gx"), lax.axis_index("gy")
    z, xh, c = gx // 4, (gx // 2) % 2, gx % 2
    y, xl = gy // 2, gy % 2
    up_y, down_y = (y + 1) % 4, (y + 3) % 4

    def along(dz=0, other_x=False, other_core=False):
        zz = (z + dz + 16) % 16
        xx = 1 - xh if other_x else xh
        cc = 1 - c if other_core else c
        return (zz * 4 + xx * 2 + cc, gy)

    def at(yy, xx):
        return (gx, yy * 2 + xx)

    loads = [pltpu.make_async_copy(s, d, load_sem.at[i]) for i, (s, d) in enumerate((
        (tok_hbm, tok_v), (grad_hbm, grad_v), (gw_hbm, gw), (uw_hbm, uw), (dw_hbm, dw)))]
    for cp in loads:
        cp.start()

    barrier = pltpu.get_barrier_semaphore()
    met = [along(dz) for dz in (8, 4, -4, 2, -2, 1, -1)]
    met += [along(dz, other_x=True) for dz in (8, 4, -4, 0)]
    met += [at(yy, xx) for yy in (up_y, down_y) for xx in (0, 1)] + [at(y, 1 - xl)]
    met += [along(other_core=True)]
    for dev in met:
        pl.semaphore_signal(barrier, inc=1, device_id=dev, device_id_type=MESH)

    loads[0].wait()
    loads[1].wait()
    first = c == 0
    tok, grad = tok_v[...].astype(F32), grad_v[...].astype(F32)
    mine = jnp.where(first, tok, grad)
    ex_out[...] = jnp.where(first, grad, tok)
    pl.semaphore_wait(barrier, len(met))

    sent = []
    marks = [0]

    def reserve(count):
        marks[0] += count
        return marks[0] - count

    def push(src, dst, dev, r=None):
        r = reserve(1) if r is None else r
        cp = pltpu.make_async_remote_copy(
            src_ref=src, dst_ref=dst, send_sem=send_sem.at[len(sent)],
            recv_sem=recv_sem.at[r], device_id=dev, device_id_type=MESH)
        cp.start()
        sent.append(cp)
        return cp

    def arrival(dst, r):
        pltpu.make_async_remote_copy(
            src_ref=dst, dst_ref=dst, send_sem=send_sem.at[0], recv_sem=recv_sem.at[r],
            device_id=at(y, 1 - xl), device_id_type=MESH).wait_recv()

    sibling = along(other_core=True)
    partner = along(other_x=True)

    push(ex_out, ex_in, sibling).wait_recv()
    theirs = ex_in[...]
    block = jnp.concatenate(
        [jnp.where(first, mine, theirs), jnp.where(first, theirs, mine)], axis=0)
    x[c, 0, 0, 0] = block.astype(BF16)

    far = [push(x.at[c, 0, 0, 0], x.at[c, 0, 0, 4 - i], along(4 * i)) for i in FAR_ORDER]
    for cp in far:
        cp.wait_recv()

    def share(n, fs):
        ours = x.at[c, n, 0, fs]
        return push(ours, ours, sibling), push(ours, x.at[c, n, 1, fs], partner)

    whole, low, high = pl.ds(0, 4), pl.ds(0, 2), pl.ds(2, 2)
    near = {3: [push(x.at[c, 0, 0, pl.ds(1, 2)], x.at[c, 3, 0, low], along(2)),
                push(x.at[c, 0, 0, high], x.at[c, 3, 0, high], along(-2))]}
    for n in (1, 2):
        near[n] = [push(x.at[c, 0, 0], x.at[c, n, 0], along(-NEAR[n]))]
    shared = {0: [(whole, share(0, whole))]}
    for n in (1, 2, 3):
        shared[n] = []
        for fs, cp in zip((whole,) if n < 3 else (low, high), near[n]):
            cp.wait_recv()
            shared[n].append((fs, share(n, fs)))

    def rows_ready(n):
        passed = []
        for fs, (from_core, from_x) in shared[n]:
            from_x.wait_recv()
            other = x.at[c, n, 1, fs]
            passed += [from_core, push(other, other, sibling)]
        for cp in passed:
            cp.wait_recv()

    b_base = [reserve(7) for _ in CHUNKS]
    c_base = [reserve(7) for _ in CHUNKS]

    def products(n):
        rows = x[0, n].reshape(128, 1024)
        part[n, :, :, 0:256] = dot(rows, gw[...], ((1,), (0,))).reshape(8, 16, 256)
        part[n, :, :, 256:512] = dot(rows, uw[...], ((1,), (0,))).reshape(8, 16, 256)
        part[n, :, :, 512:768] = dot(
            x[1, n].reshape(128, 1024), dw[...], ((1,), (1,))).reshape(8, 16, 256)
        b = b_base[n]
        across = ((y + 2) % 4) * 2
        push(part.at[n, across], b_relay.at[n, 0], at(up_y, xl), b)
        push(part.at[n, across + 1], b_relay.at[n, 1], at(down_y, xl), b + 1)
        push(part.at[n, up_y * 2 + 1], b_in.at[n, xl], at(up_y, 1), b + 2 + xl)
        push(part.at[n, down_y * 2], b_in.at[n, 2 + xl], at(down_y, 0), b + 4 + xl)
        push(part.at[n, y * 2 + 1 - xl], b_in.at[n, 4], at(y, 1 - xl), b + 6)

    def relay_sums(n):
        b = b_base[n]
        arrival(b_relay.at[n, 0], b)
        b_sum[n, 0] = b_relay[n, 0] + part[n, up_y * 2]
        push(b_sum.at[n, 0], b_in.at[n, xl], at(up_y, 0), b + 2 + xl)
        arrival(b_relay.at[n, 1], b + 1)
        b_sum[n, 1] = b_relay[n, 1] + part[n, down_y * 2 + 1]
        push(b_sum.at[n, 1], b_in.at[n, 2 + xl], at(down_y, 1), b + 4 + xl)

    def pointwise(n):
        total = part[n, gy]
        for s in range(5):
            arrival(b_in.at[n, s], b_base[n] + 2 + s)
        for s in range(5):
            total = total + b_in[n, s]
        gate, up, hgrad = total[:, 0:256], total[:, 256:512], total[:, 512:768]
        sigma = jax.nn.sigmoid(gate)
        act = gate * sigma
        h[n, gy, :, 0:256] = (act * up).astype(BF16)
        h[n, gy, :, 256:512] = (hgrad * up * sigma * (1.0 + gate * (1.0 - sigma))).astype(BF16)
        h[n, gy, :, 512:768] = (hgrad * act).astype(BF16)
        r, ours = c_base[n], h.at[n, gy]
        push(ours, ours, at(up_y, xl), r + xl)
        push(ours, ours, at(down_y, xl), r + 2 + xl)
        push(ours, ours, at(up_y, 1 - xl), r + xl)
        push(ours, ours, at(down_y, 1 - xl), r + 2 + xl)
        push(ours, ours, at(y, 1 - xl), r + 4)

    def relay_hidden(n):
        r = c_base[n]
        piece = h.at[n, down_y * 2]
        arrival(piece, r)
        push(piece, piece, at(up_y, xl), r + 5)
        piece = h.at[n, up_y * 2 + 1]
        arrival(piece, r + 3)
        push(piece, piece, at(down_y, xl), r + 6)

    def input_products(n):
        r = c_base[n]
        arrival(h.at[n, down_y * 2 + 1], r + 1)
        arrival(h.at[n, up_y * 2], r + 2)
        arrival(h.at[n, y * 2 + 1 - xl], r + 4)
        across = ((y + 2) % 4) * 2
        arrival(h.at[n, across], r + 5)
        arrival(h.at[n, across + 1], r + 6)
        hh = h[n].reshape(128, 768)
        for j in range(2):
            cols = slice(512 * j, 512 * j + 512)
            v = dot(hh[:, 256:512], gw[cols, :], ((1,), (1,)))
            v = v + dot(hh[:, 512:768], uw[cols, :], ((1,), (1,)))
            ig[n, :, :, :, cols] = v.reshape(8, 2, 8, 512)
        return push(ig.at[n, :, 1 - c], core_in.at[n], sibling)

    def send_near(n, cp):
        cp.wait_recv()
        for o in range(2):
            for f in range(4):
                v = ig[n, 4 * o + f, c] + core_in[n, 4 * o + f]
                v = jnp.concatenate([v[:, 0:512], v[:, 512:1024]], axis=0)
                if n == 0:
                    near_own[f, o] = v
                else:
                    near_out[n - 1, f, o] = v.astype(BF16)
        if n == 0:
            return []
        if n < 3:
            return [push(near_out.at[n - 1], near_in.at[n - 1], along(NEAR[n]))]
        return [push(near_out.at[2, low], near_in.at[2, low], along(2)),
                push(near_out.at[2, high], near_in.at[2, high], along(-2))]

    for cp in loads[2:]:
        cp.wait()
    core_sent = {}
    near_sent = []
    rows_ready(0)
    products(0)
    rows_ready(1)
    relay_sums(0)
    products(1)
    rows_ready(2)
    pointwise(0)
    products(2)
    relay_sums(1)
    rows_ready(3)
    relay_hidden(0)
    products(3)
    pointwise(1)
    relay_sums(2)
    core_sent[0] = input_products(0)
    relay_hidden(1)
    relay_sums(3)
    pointwise(2)
    near_sent += send_near(0, core_sent[0])
    core_sent[1] = input_products(1)
    pointwise(3)
    relay_hidden(2)
    near_sent += send_near(1, core_sent[1])
    core_sent[2] = input_products(2)
    relay_hidden(3)
    near_sent += send_near(2, core_sent[2])
    core_sent[3] = input_products(3)
    near_sent += send_near(3, core_sent[3])
    for cp in near_sent:
        cp.wait_recv()

    far_sent = []
    for f in FAR_ORDER + (0,):
        for o in range(2):
            v = near_own[f, o]
            for n in (0, 1):
                v = v + near_in[n, f, o].astype(F32)
            if f < 2:
                v = v + near_in[2, f, o].astype(F32)
            if f in (0, 3):
                v = v + near_in[2, (f + 3) % 4, o].astype(F32)
            if o == 0 and f == 0:
                near_own[f, o] = v
            else:
                far_out[f, o] = v.astype(BF16)
                far_sent.append(push(
                    far_out.at[f, o], far_in.at[f, o], along(4 * f, other_x=o == 1)))

    factor = 1.0 / jnp.sqrt(F32(512))

    @pl.loop(0, 4)
    def _(i):
        cols = pl.ds(pl.multiple_of(i * 256, 256), 256)
        hh = h[...].reshape(512, 768)
        t = x[0, :, :, :, :, cols].reshape(512, 256)
        gg_v[cols, :] = (dot(t, hh[:, 256:512], ((0,), (0,))) * factor).astype(BF16)
        ug_v[cols, :] = (dot(t, hh[:, 512:768], ((0,), (0,))) * factor).astype(BF16)
        g = x[1, :, :, :, :, cols].reshape(512, 256)
        dg_v[:, cols] = (dot(hh[:, 0:256], g, ((0,), (0,))) * factor).astype(BF16)

    stores = [pltpu.make_async_copy(s, d, store_sem.at[i]) for i, (s, d) in enumerate((
        (gg_v, gg_hbm), (ug_v, ug_hbm), (dg_v, dg_hbm), (ig_v, ig_hbm)))]
    for cp in stores[:3]:
        cp.start()
    for cp in far_sent:
        cp.wait_recv()
    v = near_own[0, 0] + far_in[0, 1].astype(F32)
    for f in (1, 2, 3):
        v = v + (far_in[f, 0].astype(F32) + far_in[f, 1].astype(F32))
    ig_v[...] = jnp.concatenate([v[0:8], v[8:16]], axis=1).astype(BF16)
    stores[3].start()
    for cp in sent:
        cp.wait_send()
    for cp in stores:
        cp.wait()


def place(a, b, c, d, ao, bo, co, do, sem):
    copies = [pltpu.make_async_copy(s, t, sem.at[i])
              for i, (s, t) in enumerate(((b, bo), (c, co), (d, do), (a, ao)))]
    for cp in copies:
        cp.start()
    for cp in copies:
        cp.wait()


def per_device(tokens, out_grad, gate_weight, up_weight, down_weight):
    hbm = pl.BlockSpec(memory_space=pl.ANY)
    shape = jax.ShapeDtypeStruct
    outs = (shape((8, 1024), BF16), shape((1024, 256), BF16),
            shape((1024, 256), BF16), shape((256, 1024), BF16))
    results = pl.pallas_call(
        kernel,
        out_shape=outs,
        in_specs=[hbm] * 5,
        out_specs=(hbm,) * 4,
        scratch_shapes=[
            pltpu.VMEM((8, 1024), BF16),
            pltpu.VMEM((8, 1024), BF16),
            pltpu.VMEM((1024, 256), BF16),
            pltpu.VMEM((1024, 256), BF16),
            pltpu.VMEM((256, 1024), BF16),
            pltpu.VMEM((8, 1024), F32),
            pltpu.VMEM((8, 1024), F32),
            pltpu.VMEM((2, 4, 2, 4, 16, 1024), BF16),
            pltpu.VMEM((4, 8, 16, 768), F32),
            pltpu.VMEM((4, 2, 16, 768), F32),
            pltpu.VMEM((4, 2, 16, 768), F32),
            pltpu.VMEM((4, 5, 16, 768), F32),
            pltpu.VMEM((4, 8, 16, 768), BF16),
            pltpu.VMEM((4, 8, 2, 8, 1024), F32),
            pltpu.VMEM((4, 8, 8, 1024), F32),
            pltpu.VMEM((3, 4, 2, 16, 512), BF16),
            pltpu.VMEM((4, 2, 16, 512), F32),
            pltpu.VMEM((3, 4, 2, 16, 512), BF16),
            pltpu.VMEM((4, 2, 16, 512), BF16),
            pltpu.VMEM((4, 2, 16, 512), BF16),
            pltpu.VMEM((8, 1024), BF16),
            pltpu.VMEM((1024, 256), BF16),
            pltpu.VMEM((1024, 256), BF16),
            pltpu.VMEM((256, 1024), BF16),
            pltpu.SemaphoreType.DMA((5,)),
            pltpu.SemaphoreType.DMA((4,)),
            pltpu.SemaphoreType.DMA((COPIES,)),
            pltpu.SemaphoreType.DMA((COPIES,)),
        ],
        compiler_params=pltpu.CompilerParams(
            collective_id=0, has_side_effects=True, vmem_limit_bytes=60 << 20),
        cost_estimate=pl.CostEstimate(
            flops=2 * 8 * 512 * 1024 * 256, bytes_accessed=4 << 20, transcendentals=64 * 256),
    )(tokens, out_grad, gate_weight, up_weight, down_weight)
    return pl.pallas_call(
        place,
        out_shape=outs,
        in_specs=[hbm] * 4,
        out_specs=(hbm,) * 4,
        scratch_shapes=[pltpu.SemaphoreType.DMA((4,))],
    )(*results)


def solution(mesh):
    return jax.shard_map(
        per_device,
        mesh=mesh,
        in_specs=(P("gx", "gy"), P("gx", "gy"), P("gy", "gx"), P("gy", "gx"), P("gx", "gy")),
        out_specs=(P("gx", "gy"), P("gy", "gx"), P("gy", "gx"), P("gx", "gy")),
        check_vma=False,
    )
```

time: 103 us -> 142 us (1.38)
  Pallas kernels: 94.1 us -> 140 us
  local copies, waits for them, and re-layouts: 7.54 us -> 0 us
    pallas_call x1 -> x2, Pallas kernels: 94.1 us -> 140 us  [the longest x1 91.2 us: per_device(): pl.pallas_call(kernel, out_shape=outs, in_specs=[hbm] * 5, out_specs=(hbm...]
    unnamed x14 -> x0, local copies, waits for them, and re-layouts: 7.54 us -> none
where the time goes in v2:
time: 142 us; the launch traced here: 141 us
  Pallas kernels  140 us (99%)
    pallas_call x1, Pallas kernels, per_device(): pl.pallas_call(kernel, out_shape=outs, in_specs=[hbm] * 5, out_specs=(hbm...  91.2 us
    pallas_call x1, Pallas kernels, per_device(): pl.pallas_call(place, out_shape=outs, in_specs=[hbm] * 4, out_specs=(hbm,...  49.3 us

profile of v2, /device:TPU:1, one launch (start us, length us, event | category | flops | bytes accessed | tf_op | source)
XLA Modules:
  0.0 141.1 jit_solution(13307017531344712128)
XLA Ops:
  0.6 91.2 %shard_map.84 = (bf16[8,1024]{1,0:T(8,128)(2,1)}, bf16[1024,256]{1,0:T(8,128)(2,1)}, bf16[1024,256]{1,0:T(8,128)(2,1)}, bf16[256,1024]{1,0:T(8,128)(2,1)}) custom-call(bf16[8,1024]{1,0:T(8,128)(2,1)} %tok_hbm.1, bf16[8,1024]{1,0:T(8,128)(2,1)} %grad_hbm.1, bf16[1024,256]{1,0:T(8,128)(2,1)} %gw_hbm.1, bf16[1024,256]{1,0:T(8,128)(2,1)} %uw_hbm.1, ...), custom_call_target="tpu_custom_call" | custom-call | flops 2147483648 | bytes 4194304 | tf_op jit(solution)/shard_map/pallas_call | solution.py:303
  91.8 49.3 %shard_map.85 = (bf16[8,1024]{1,0:T(8,128)(2,1)}, bf16[1024,256]{1,0:T(8,128)(2,1)}, bf16[1024,256]{1,0:T(8,128)(2,1)}, bf16[256,1024]{1,0:T(8,128)(2,1)}) custom-call(bf16[8,1024]{1,0:T(8,128)(2,1)} %get-tuple-element.8.a, bf16[1024,256]{1,0:T(8,128)(2,1)} %get-tuple-element.9.b, bf16[1024,256]{1,0:T(8,128)(2,1)} %get-tuple-element.10.c, ...), custom_call_target="tpu_custom_call" | custom-call | tf_op jit(solution)/shard_map/pallas_call | solution.py:343

commit v3 on v1

--- a/solution.py
+++ b/solution.py
@@ -10,18 +10,19 @@
 
 NEAR = (0, 1, -1, 2)
 FAR_ORDER = (2, 1, 3)
-NEAR_ORDER = (3, 1, 2)
 
 
 def dot(a, b, dims):
     return lax.dot_general(a, b, (dims, ((), ())), preferred_element_type=F32)
 
 
-def kernel(tok_ref, grad_ref, gw_hbm, uw_hbm, dw_hbm,
+def kernel(tok_hbm, grad_hbm, gw_hbm, uw_hbm, dw_hbm,
+           ig_hbm, gg_hbm, ug_hbm, dg_hbm,
+           tok_ref, grad_ref, gw, uw, dw, ex_out, ex_in, x, part, part_low, gate_part, gate_in, b_in, h,
+           ig, core_in,
+           near_out, near_own, near_in, far_out, far_in,
            ig_ref, gg_ref, ug_ref, dg_ref,
-           gw, uw, dw, ex_out, ex_in, x, part, b_in, h, ig, core_in,
-           near_out, near_own, near_in, far_out, far_in,
-           w_sem, send_sem, recv_sem):
+           load_sem, store_sem, send_sem, recv_sem):
     gx, gy = lax.axis_index("gx"), lax.axis_index("gy")
     z, xh, c = gx // 4, (gx // 2) % 2, gx % 2
     y, xl = gy // 2, gy % 2
@@ -37,8 +38,8 @@
     def across(dy, dx):
         return ((y + dy) % 4) * 2 + (xl + dx) % 2
 
-    loads = [pltpu.make_async_copy(s, d, w_sem.at[i])
-             for i, (s, d) in enumerate(((gw_hbm, gw), (uw_hbm, uw), (dw_hbm, dw)))]
+    loads = [pltpu.make_async_copy(s, d, load_sem.at[i]) for i, (s, d) in enumerate((
+        (tok_hbm, tok_ref), (grad_hbm, grad_ref), (gw_hbm, gw), (uw_hbm, uw), (dw_hbm, dw)))]
     for cp in loads:
         cp.start()
 
@@ -50,6 +51,8 @@
     for dev in met:
         pl.semaphore_signal(barrier, inc=1, device_id=dev, device_id_type=MESH)
 
+    loads[0].wait()
+    loads[1].wait()
     first = c == 0
     tok, grad = tok_ref[...].astype(F32), grad_ref[...].astype(F32)
     mine = jnp.where(first, tok, grad)
@@ -79,30 +82,43 @@
     far = [push(x.at[c, 0, 0, 0], x.at[c, 0, 0, 4 - i], along(4 * i)) for i in FAR_ORDER]
     for cp in far:
         cp.wait_recv()
-    near = [push(x.at[c, 0, 0], x.at[c, 0, n], along(-NEAR[n])) for n in NEAR_ORDER]
-    to_x = [push(x.at[c, 0, 0], x.at[c, 1, 0], partner)]
-    to_core = [push(x.at[c, 0, 0], x.at[c, 0, 0], sibling)]
-    for n, cp in zip((1, 2, 3), (near[1], near[2], near[0])):
+    whole, low, high = pl.ds(0, 4), pl.ds(0, 2), pl.ds(2, 2)
+
+    def share(n, fs):
+        ours = x.at[c, 0, n, fs]
+        return push(ours, ours, sibling), push(ours, x.at[c, 1, n, fs], partner), fs, n
+
+    near = [(3, low, push(x.at[c, 0, 0, pl.ds(1, 2)], x.at[c, 0, 3, low], along(2))),
+            (3, high, push(x.at[c, 0, 0, high], x.at[c, 0, 3, high], along(-2)))]
+    near = [(n, whole, push(x.at[c, 0, 0], x.at[c, 0, n], along(-NEAR[n]))) for n in (1, 2)] + near
+    shared = [share(0, whole)]
+    for n, fs, cp in near:
         cp.wait_recv()
-        to_x.append(push(x.at[c, 0, n], x.at[c, 1, n], partner))
-        to_core.append(push(x.at[c, 0, n], x.at[c, 0, n], sibling))
+        shared.append(share(n, fs))
 
     def products(k):
         rows = x[0, k].reshape(256, 1024)
-        part[k, :, :, 0:256] = dot(rows, gw[...], ((1,), (0,))).reshape(8, 32, 256)
-        part[k, :, :, 256:512] = dot(rows, uw[...], ((1,), (0,))).reshape(8, 32, 256)
-        part[k, :, :, 512:768] = dot(
-            x[1, k].reshape(256, 1024), dw[...], ((1,), (1,))).reshape(8, 32, 256)
-        return [push(part.at[k, across(dy, dx)], b_in.at[k, s], (gx, across(dy, dx)))
+        up = dot(rows, uw[...], ((1,), (0,))).reshape(8, 32, 256)
+        hgrad = dot(x[1, k].reshape(256, 1024), dw[...], ((1,), (1,))).reshape(8, 32, 256)
+        part_low[k, :, :, 0:256] = up.astype(BF16)
+        part_low[k, :, :, 256:512] = hgrad.astype(BF16)
+        part[k, :, :, 0:256] = up
+        part[k, :, :, 256:512] = hgrad
+        sums = [push(part_low.at[k, across(dy, dx)], b_in.at[k, s], (gx, across(dy, dx)))
                 for s, (dy, dx) in enumerate(peers)]
+        gate = dot(rows, gw[...], ((1,), (0,))).reshape(8, 32, 256)
+        gate_part[k] = gate
+        return sums + [push(gate_part.at[k, across(dy, dx)], gate_in.at[k, s], (gx, across(dy, dx)))
+                       for s, (dy, dx) in enumerate(peers)]
 
     def pointwise(k, arrived):
         for cp in arrived:
             cp.wait_recv()
-        total = part[k, gy]
+        total, gate = part[k, gy], gate_part[k, gy]
         for s in range(7):
-            total = total + b_in[k, s]
-        gate, up, hgrad = total[:, 0:256], total[:, 256:512], total[:, 512:768]
+            total = total + b_in[k, s].astype(F32)
+            gate = gate + gate_in[k, s]
+        up, hgrad = total[:, 0:256], total[:, 256:512]
         sigma = jax.nn.sigmoid(gate)
         act = gate * sigma
         h[k, gy, :, 0:256] = (act * up).astype(BF16)
@@ -132,15 +148,21 @@
                     near_own[k, f] = v
                 else:
                     near_out[k, n, f] = v.astype(BF16)
-        return [push(near_out.at[k, n], near_in.at[k, n], along(NEAR[n])) for n in NEAR_ORDER]
+        two = [push(near_out.at[k, 3, fs], near_in.at[k, 3, fs], along(dz))
+               for fs, dz in ((low, 2), (high, -2))]
+        return two + [push(near_out.at[k, n], near_in.at[k, n], along(NEAR[n])) for n in (1, 2)]
 
     def send_far(k, arrived):
         for cp in arrived:
             cp.wait_recv()
         for f in range(4):
             v = near_own[k, f]
-            for n in (1, 2, 3):
+            for n in (1, 2):
                 v = v + near_in[k, n, f].astype(F32)
+            if f < 2:
+                v = v + near_in[k, 3, f].astype(F32)
+            if f in (0, 3):
+                v = v + near_in[k, 3, (f + 3) % 4].astype(F32)
             if k == 0 and f == 0:
                 near_own[k, f] = v
             else:
@@ -149,16 +171,17 @@
         return [push(far_out.at[k, f], far_in.at[k, f], along(4 * f, other_x=k == 1))
                 for f in order]
 
-    for cp in loads:
+    for cp in loads[2:]:
         cp.wait()
-    for cp in to_core:
-        cp.wait_recv()
+    for from_core, _, _, _ in shared:
+        from_core.wait_recv()
     b0 = products(0)
 
     to_core = []
-    for n in range(4):
-        to_x[n].wait_recv()
-        to_core.append(push(x.at[c, 1, n], x.at[c, 1, n], sibling))
+    for _, from_x, fs, n in shared:
+        from_x.wait_recv()
+        other = x.at[c, 1, n, fs]
+        to_core.append(push(other, other, sibling))
     for cp in to_core:
         cp.wait_recv()
     b1 = products(1)
@@ -184,6 +207,10 @@
         g = x[1, :, :, :, :, cols].reshape(512, 256)
         dg_ref[:, cols] = (dot(hh[:, 0:256], g, ((0,), (0,))) * factor).astype(BF16)
 
+    stores = [pltpu.make_async_copy(s, d, store_sem.at[i]) for i, (s, d) in enumerate((
+        (gg_ref, gg_hbm), (ug_ref, ug_hbm), (dg_ref, dg_hbm), (ig_ref, ig_hbm)))]
+    for cp in stores[:3]:
+        cp.start()
     for cp in f0 + f1:
         cp.wait_recv()
     v = near_own[0, 0] + far_in[1, 0].astype(F32)
@@ -191,32 +218,55 @@
         v = v + (far_in[0, f].astype(F32) + far_in[1, f].astype(F32))
     ig_ref[...] = jnp.concatenate([v[0:8], v[8:16]], axis=1).astype(BF16)
 
+    stores[3].start()
     for cp in sent:
         cp.wait_send()
-
-
-COPIES = 62
+    for cp in stores:
+        cp.wait()
+
+
+COPIES = 86
+
+
+def place(*refs):
+    given, wanted, held, load_sem, store_sem = refs[:4], refs[4:8], refs[8:12], refs[12], refs[13]
+    loads = [pltpu.make_async_copy(s, v, load_sem.at[i])
+             for i, (s, v) in enumerate(zip(given, held))]
+    stores = [pltpu.make_async_copy(v, d, store_sem.at[i])
+              for i, (v, d) in enumerate(zip(held, wanted))]
+    for cp in loads:
+        cp.start()
+    for load, store in zip(loads, stores):
+        load.wait()
+        store.start()
+    for cp in stores:
+        cp.wait()
 
 
 def per_device(tokens, out_grad, gate_weight, up_weight, down_weight):
-    vmem = pl.BlockSpec(memory_space=pltpu.VMEM)
     hbm = pl.BlockSpec(memory_space=pl.ANY)
     shape = jax.ShapeDtypeStruct
-    return pl.pallas_call(
+    outs = (shape((8, 1024), BF16), shape((1024, 256), BF16),
+            shape((1024, 256), BF16), shape((256, 1024), BF16))
+    results = pl.pallas_call(
         kernel,
-        out_shape=(shape((8, 1024), BF16), shape((1024, 256), BF16),
-                   shape((1024, 256), BF16), shape((256, 1024), BF16)),
-        in_specs=[vmem, vmem, hbm, hbm, hbm],
-        out_specs=(vmem,) * 4,
+        out_shape=outs,
+        in_specs=[hbm] * 5,
+        out_specs=(hbm,) * 4,
         scratch_shapes=[
+            pltpu.VMEM((8, 1024), BF16),
+            pltpu.VMEM((8, 1024), BF16),
             pltpu.VMEM((1024, 256), BF16),
             pltpu.VMEM((1024, 256), BF16),
             pltpu.VMEM((256, 1024), BF16),
             pltpu.VMEM((8, 1024), F32),
             pltpu.VMEM((8, 1024), F32),
             pltpu.VMEM((2, 2, 4, 4, 16, 1024), BF16),
-            pltpu.VMEM((2, 8, 32, 768), F32),
-            pltpu.VMEM((2, 7, 32, 768), F32),
+            pltpu.VMEM((2, 8, 32, 512), F32),
+            pltpu.VMEM((2, 8, 32, 512), BF16),
+            pltpu.VMEM((2, 8, 32, 256), F32),
+            pltpu.VMEM((2, 7, 32, 256), F32),
+            pltpu.VMEM((2, 7, 32, 512), BF16),
             pltpu.VMEM((2, 8, 32, 768), BF16),
             pltpu.VMEM((2, 16, 2, 8, 1024), F32),
             pltpu.VMEM((2, 16, 8, 1024), F32),
@@ -225,15 +275,29 @@
             pltpu.VMEM((2, 4, 4, 16, 512), BF16),
             pltpu.VMEM((2, 4, 16, 512), BF16),
             pltpu.VMEM((2, 4, 16, 512), BF16),
-            pltpu.SemaphoreType.DMA((3,)),
+            pltpu.VMEM((8, 1024), BF16),
+            pltpu.VMEM((1024, 256), BF16),
+            pltpu.VMEM((1024, 256), BF16),
+            pltpu.VMEM((256, 1024), BF16),
+            pltpu.SemaphoreType.DMA((5,)),
+            pltpu.SemaphoreType.DMA((4,)),
             pltpu.SemaphoreType.DMA((COPIES,)),
             pltpu.SemaphoreType.DMA((COPIES,)),
         ],
         compiler_params=pltpu.CompilerParams(
-            collective_id=0, has_side_effects=True, vmem_limit_bytes=48 << 20),
+            collective_id=0, has_side_effects=True, vmem_limit_bytes=60 << 20),
         cost_estimate=pl.CostEstimate(
             flops=2 * 8 * 512 * 1024 * 256, bytes_accessed=4 << 20, transcendentals=64 * 256),
     )(tokens, out_grad, gate_weight, up_weight, down_weight)
+    return pl.pallas_call(
+        place,
+        out_shape=outs,
+        in_specs=[hbm] * 4,
+        out_specs=(hbm,) * 4,
+        scratch_shapes=[pltpu.VMEM(o.shape, BF16) for o in outs]
+        + [pltpu.SemaphoreType.DMA((4,))] * 2,
+        compiler_params=pltpu.CompilerParams(vmem_limit_bytes=60 << 20),
+    )(*results)
 
 
 def solution(mesh):

time: 103 us -> 89.7 us (0.87)
  local copies, waits for them, and re-layouts: 7.54 us -> 0 us
  Pallas kernels: 94.1 us -> 88.8 us
    unnamed x14 -> x0, local copies, waits for them, and re-layouts: 7.54 us -> none
    pallas_call x1 -> x2, Pallas kernels: 94.1 us -> 88.8 us  [the longest x1 86.5 us: per_device(): pl.pallas_call(kernel, out_shape=outs, in_specs=[hbm] * 5, out_specs=(hbm...]
where the time goes in v3:
time: 89.7 us; the launch traced here: 89.5 us
  Pallas kernels  88.8 us (99%)
    pallas_call x1, Pallas kernels, per_device(): pl.pallas_call(kernel, out_shape=outs, in_specs=[hbm] * 5, out_specs=(hbm...  86.5 us
    pallas_call x1, Pallas kernels, per_device(): pl.pallas_call(place, out_shape=outs, in_specs=[hbm] * 4, out_specs=(hbm,...  2.27 us

profile of v3, /device:TPU:1, one launch (start us, length us, event | category | flops | bytes accessed | tf_op | source)
XLA Modules:
  0.0 89.5 jit_solution(17150418556538779082)
XLA Ops:
  0.6 86.5 %shard_map.84 = (bf16[8,1024]{1,0:T(8,128)(2,1)}, bf16[1024,256]{1,0:T(8,128)(2,1)}, bf16[1024,256]{1,0:T(8,128)(2,1)}, bf16[256,1024]{1,0:T(8,128)(2,1)}) custom-call(bf16[8,1024]{1,0:T(8,128)(2,1)} %tok_hbm.1, bf16[8,1024]{1,0:T(8,128)(2,1)} %grad_hbm.1, bf16[1024,256]{1,0:T(8,128)(2,1)} %gw_hbm.1, bf16[1024,256]{1,0:T(8,128)(2,1)} %uw_hbm.1, ...), custom_call_target="tpu_custom_call" | custom-call | flops 2147483648 | bytes 4194304 | tf_op jit(solution)/shard_map/pallas_call | solution.py:251
  87.2 2.3 %shard_map.85 = (bf16[8,1024]{1,0:T(8,128)(2,1)}, bf16[1024,256]{1,0:T(8,128)(2,1)}, bf16[1024,256]{1,0:T(8,128)(2,1)}, bf16[256,1024]{1,0:T(8,128)(2,1)}) custom-call(bf16[8,1024]{1,0:T(8,128)(2,1)} %get-tuple-element.8.refs_0_, bf16[1024,256]{1,0:T(8,128)(2,1)} %get-tuple-element.9.refs_1_, bf16[1024,256]{1,0:T(8,128)(2,1)} %get-tuple-element.10.refs_2_, ...), custom_call_target="tpu_custom_call" | custom-call | tf_op jit(solution)/shard_map/pallas_call | solution.py:292

commit v4 on v3

--- a/solution.py
+++ b/solution.py
@@ -10,6 +10,7 @@
 
 NEAR = (0, 1, -1, 2)
 FAR_ORDER = (2, 1, 3)
+PLACE = (1, 2, 0, 3)
 
 
 def dot(a, b, dims):
@@ -79,22 +80,37 @@
         [jnp.where(first, mine, theirs), jnp.where(first, theirs, mine)], axis=0)
     x[c, 0, 0, 0] = block.astype(BF16)
 
-    far = [push(x.at[c, 0, 0, 0], x.at[c, 0, 0, 4 - i], along(4 * i)) for i in FAR_ORDER]
-    for cp in far:
-        cp.wait_recv()
-    whole, low, high = pl.ds(0, 4), pl.ds(0, 2), pl.ds(2, 2)
-
-    def share(n, fs):
-        ours = x.at[c, 0, n, fs]
-        return push(ours, ours, sibling), push(ours, x.at[c, 1, n, fs], partner), fs, n
-
-    near = [(3, low, push(x.at[c, 0, 0, pl.ds(1, 2)], x.at[c, 0, 3, low], along(2))),
-            (3, high, push(x.at[c, 0, 0, high], x.at[c, 0, 3, high], along(-2)))]
-    near = [(n, whole, push(x.at[c, 0, 0], x.at[c, 0, n], along(-NEAR[n]))) for n in (1, 2)] + near
-    shared = [share(0, whole)]
-    for n, fs, cp in near:
-        cp.wait_recv()
-        shared.append(share(n, fs))
+    shared, arriving = [], {}
+
+    def share(n, f):
+        ours = x.at[c, 0, n, f]
+        from_x = push(ours, x.at[c, 1, n, f], partner)
+        shared.append((push(ours, ours, sibling), from_x, n, f))
+
+    def to_near(f):
+        ours = x.at[c, 0, 0, f]
+        if f < 2:
+            arriving[3, f] = push(ours, x.at[c, 0, 3, f], along(-2))
+        if f in (0, 3):
+            arriving[3, (f + 3) % 4] = push(ours, x.at[c, 0, 3, (f + 3) % 4], along(2))
+        for n in (1, 2):
+            arriving[n, f] = push(ours, x.at[c, 0, n, f], along(-NEAR[n]))
+
+    def pass_on(*slots):
+        for slot in slots:
+            arriving.pop(slot).wait_recv()
+            share(*slot)
+
+    for i in FAR_ORDER:
+        arriving[0, 4 - i] = push(x.at[c, 0, 0, 0], x.at[c, 0, 0, 4 - i], along(4 * i))
+    to_near(0)
+    share(0, 0)
+    pass_on((1, 0), (2, 0), (3, 0), (3, 3))
+    for f in (1, 3, 2):
+        arriving.pop((0, f)).wait_recv()
+        to_near(f)
+        share(0, f)
+    pass_on((1, 1), (2, 1), (3, 1), (1, 3), (2, 3), (3, 2), (1, 2), (2, 2))
 
     def products(k):
         rows = x[0, k].reshape(256, 1024)
@@ -147,18 +163,26 @@
                 if n == 0:
                     near_own[k, f] = v
                 else:
-                    near_out[k, n, f] = v.astype(BF16)
-        two = [push(near_out.at[k, 3, fs], near_in.at[k, 3, fs], along(dz))
-               for fs, dz in ((low, 2), (high, -2))]
-        return two + [push(near_out.at[k, n], near_in.at[k, n], along(NEAR[n])) for n in (1, 2)]
-
-    def send_far(k, arrived):
-        for cp in arrived:
+                    near_out[k, n, f if n == 3 else PLACE[f]] = v.astype(BF16)
+
+        def to(n, fs, dz):
+            return push(near_out.at[k, n, fs], near_in.at[k, n, fs], along(dz))
+
+        early = [to(n, pl.ds(0, 1), NEAR[n]) for n in (1, 2)]
+        late = [to(3, pl.ds(0, 2), 2), to(3, pl.ds(2, 2), -2)]
+        return early, late + [to(n, pl.ds(1, 3), NEAR[n]) for n in (1, 2)]
+
+    def send_far(k, early, late):
+        out = []
+        for cp in early:
             cp.wait_recv()
-        for f in range(4):
+        for f in FAR_ORDER + (0,):
+            if f == FAR_ORDER[1]:
+                for cp in late:
+                    cp.wait_recv()
             v = near_own[k, f]
             for n in (1, 2):
-                v = v + near_in[k, n, f].astype(F32)
+                v = v + near_in[k, n, PLACE[f]].astype(F32)
             if f < 2:
                 v = v + near_in[k, 3, f].astype(F32)
             if f in (0, 3):
@@ -167,9 +191,9 @@
                 near_own[k, f] = v
             else:
                 far_out[k, f] = v.astype(BF16)
-        order = FAR_ORDER if k == 0 else FAR_ORDER + (0,)
-        return [push(far_out.at[k, f], far_in.at[k, f], along(4 * f, other_x=k == 1))
-                for f in order]
+                out.append(push(far_out.at[k, f], far_in.at[k, f],
+                                along(4 * f, other_x=k == 1)))
+        return out
 
     for cp in loads[2:]:
         cp.wait()
@@ -178,9 +202,9 @@
     b0 = products(0)
 
     to_core = []
-    for _, from_x, fs, n in shared:
+    for _, from_x, n, f in shared:
         from_x.wait_recv()
-        other = x.at[c, 1, n, fs]
+        other = x.at[c, 1, n, f]
         to_core.append(push(other, other, sibling))
     for cp in to_core:
         cp.wait_recv()
@@ -192,8 +216,8 @@
     n0 = send_near(0, i0)
     i1 = input_products(1, c1)
     n1 = send_near(1, i1)
-    f0 = send_far(0, n0)
-    f1 = send_far(1, n1)
+    f0 = send_far(0, *n0)
+    f1 = send_far(1, *n1)
 
     factor = 1.0 / jnp.sqrt(F32(512))
 
@@ -225,7 +249,7 @@
         cp.wait()
 
 
-COPIES = 86
+COPIES = 128
 
 
 def place(*refs):

time: 89.7 us -> 83.4 us (0.930)
  Pallas kernels: 88.8 us -> 82.5 us
    pallas_call x1, Pallas kernels: 86.5 us -> 80.2 us  [per_device(): pl.pallas_call(kernel, out_shape=outs, in_specs=[hbm] * 5, out_specs=(hbm...]
where the time goes in v4:
time: 83.4 us; the launch traced here: 83.1 us
  Pallas kernels  82.5 us (99%)
    pallas_call x1, Pallas kernels, per_device(): pl.pallas_call(kernel, out_shape=outs, in_specs=[hbm] * 5, out_specs=(hbm...  80.2 us
    pallas_call x1, Pallas kernels, per_device(): pl.pallas_call(place, out_shape=outs, in_specs=[hbm] * 4, out_specs=(hbm,...  2.27 us

profile of v4, /device:TPU:1, one launch (start us, length us, event | category | flops | bytes accessed | tf_op | source)
XLA Modules:
  0.0 83.1 jit_solution(12575782239545318528)
XLA Ops:
  0.6 80.2 %shard_map.84 = (bf16[8,1024]{1,0:T(8,128)(2,1)}, bf16[1024,256]{1,0:T(8,128)(2,1)}, bf16[1024,256]{1,0:T(8,128)(2,1)}, bf16[256,1024]{1,0:T(8,128)(2,1)}) custom-call(bf16[8,1024]{1,0:T(8,128)(2,1)} %tok_hbm.1, bf16[8,1024]{1,0:T(8,128)(2,1)} %grad_hbm.1, bf16[1024,256]{1,0:T(8,128)(2,1)} %gw_hbm.1, bf16[1024,256]{1,0:T(8,128)(2,1)} %uw_hbm.1, ...), custom_call_target="tpu_custom_call" | custom-call | flops 2147483648 | bytes 4194304 | tf_op jit(solution)/shard_map/pallas_call | solution.py:275
  80.9 2.3 %shard_map.85 = (bf16[8,1024]{1,0:T(8,128)(2,1)}, bf16[1024,256]{1,0:T(8,128)(2,1)}, bf16[1024,256]{1,0:T(8,128)(2,1)}, bf16[256,1024]{1,0:T(8,128)(2,1)}) custom-call(bf16[8,1024]{1,0:T(8,128)(2,1)} %get-tuple-element.8.refs_0_, bf16[1024,256]{1,0:T(8,128)(2,1)} %get-tuple-element.9.refs_1_, bf16[1024,256]{1,0:T(8,128)(2,1)} %get-tuple-element.10.refs_2_, ...), custom_call_target="tpu_custom_call" | custom-call | tf_op jit(solution)/shard_map/pallas_call | solution.py:316

commit v5 on v4

--- a/solution.py
+++ b/solution.py
@@ -19,7 +19,7 @@
 
 def kernel(tok_hbm, grad_hbm, gw_hbm, uw_hbm, dw_hbm,
            ig_hbm, gg_hbm, ug_hbm, dg_hbm,
-           tok_ref, grad_ref, gw, uw, dw, ex_out, ex_in, x, part, part_low, gate_part, gate_in, b_in, h,
+           tok_ref, grad_ref, gw, uw, dw, ex_out, ex_in, x, part, part_low, gate_part, gate_in, b_in, h, hidden,
            ig, core_in,
            near_out, near_own, near_in, far_out, far_in,
            ig_ref, gg_ref, ug_ref, dg_ref,
@@ -137,19 +137,22 @@
         up, hgrad = total[:, 0:256], total[:, 256:512]
         sigma = jax.nn.sigmoid(gate)
         act = gate * sigma
-        h[k, gy, :, 0:256] = (act * up).astype(BF16)
-        h[k, gy, :, 256:512] = (hgrad * up * sigma * (1.0 + gate * (1.0 - sigma))).astype(BF16)
-        h[k, gy, :, 512:768] = (hgrad * act).astype(BF16)
-        return [push(h.at[k, gy], h.at[k, gy], (gx, across(dy, dx))) for dy, dx in peers]
+        h[k, gy, :, 0:256] = (hgrad * up * sigma * (1.0 + gate * (1.0 - sigma))).astype(BF16)
+        h[k, gy, :, 256:512] = (hgrad * act).astype(BF16)
+        hidden[k, gy] = (act * up).astype(BF16)
+        return spread(k, h)
+
+    def spread(k, ref):
+        return [push(ref.at[k, gy], ref.at[k, gy], (gx, across(dy, dx))) for dy, dx in peers]
 
     def input_products(k, arrived):
         for cp in arrived:
             cp.wait_recv()
-        hh = h[k].reshape(256, 768)
+        hh = h[k].reshape(256, 512)
         for j in range(2):
             cols = slice(512 * j, 512 * j + 512)
-            v = dot(hh[:, 256:512], gw[cols, :], ((1,), (1,)))
-            v = v + dot(hh[:, 512:768], uw[cols, :], ((1,), (1,)))
+            v = dot(hh[:, 0:256], gw[cols, :], ((1,), (1,)))
+            v = v + dot(hh[:, 256:512], uw[cols, :], ((1,), (1,)))
             ig[k, :, :, :, cols] = v.reshape(16, 2, 8, 512)
         return push(ig.at[k, :, 1 - c], core_in.at[k], sibling)
 
@@ -214,27 +217,34 @@
     c1 = pointwise(1, b1)
     i0 = input_products(0, c0)
     n0 = send_near(0, i0)
+    spread_hidden = spread(0, hidden)
     i1 = input_products(1, c1)
     n1 = send_near(1, i1)
+    spread_hidden += spread(1, hidden)
     f0 = send_far(0, *n0)
     f1 = send_far(1, *n1)
 
+    for cp in spread_hidden:
+        cp.wait_recv()
     factor = 1.0 / jnp.sqrt(F32(512))
 
     @pl.loop(0, 4)
     def _(i):
         cols = pl.ds(pl.multiple_of(i * 256, 256), 256)
-        hh = h[...].reshape(512, 768)
+        hh = h[...].reshape(512, 512)
         t = x[0, :, :, :, :, cols].reshape(512, 256)
-        gg_ref[cols, :] = (dot(t, hh[:, 256:512], ((0,), (0,))) * factor).astype(BF16)
-        ug_ref[cols, :] = (dot(t, hh[:, 512:768], ((0,), (0,))) * factor).astype(BF16)
+        gg_ref[cols, :] = (dot(t, hh[:, 0:256], ((0,), (0,))) * factor).astype(BF16)
+        ug_ref[cols, :] = (dot(t, hh[:, 256:512], ((0,), (0,))) * factor).astype(BF16)
         g = x[1, :, :, :, :, cols].reshape(512, 256)
-        dg_ref[:, cols] = (dot(hh[:, 0:256], g, ((0,), (0,))) * factor).astype(BF16)
+        dg_ref[:, cols] = (dot(
+            hidden[...].reshape(512, 256), g, ((0,), (0,))) * factor).astype(BF16)
 
     stores = [pltpu.make_async_copy(s, d, store_sem.at[i]) for i, (s, d) in enumerate((
         (gg_ref, gg_hbm), (ug_ref, ug_hbm), (dg_ref, dg_hbm), (ig_ref, ig_hbm)))]
     for cp in stores[:3]:
         cp.start()
+    for cp in sent:
+        cp.wait_send()
     for cp in f0 + f1:
         cp.wait_recv()
     v = near_own[0, 0] + far_in[1, 0].astype(F32)
@@ -243,13 +253,11 @@
     ig_ref[...] = jnp.concatenate([v[0:8], v[8:16]], axis=1).astype(BF16)
 
     stores[3].start()
-    for cp in sent:
-        cp.wait_send()
     for cp in stores:
         cp.wait()
 
 
-COPIES = 128
+COPIES = 144
 
 
 def place(*refs):
@@ -291,7 +299,8 @@
             pltpu.VMEM((2, 8, 32, 256), F32),
             pltpu.VMEM((2, 7, 32, 256), F32),
             pltpu.VMEM((2, 7, 32, 512), BF16),
-            pltpu.VMEM((2, 8, 32, 768), BF16),
+            pltpu.VMEM((2, 8, 32, 512), BF16),
+            pltpu.VMEM((2, 8, 32, 256), BF16),
             pltpu.VMEM((2, 16, 2, 8, 1024), F32),
             pltpu.VMEM((2, 16, 8, 1024), F32),
             pltpu.VMEM((2, 4, 4, 16, 512), BF16),

time: 83.4 us -> 80.7 us (0.968)
  Pallas kernels: 82.5 us -> 79.8 us
    pallas_call x1, Pallas kernels: 80.2 us -> 77.5 us  [per_device(): pl.pallas_call(kernel, out_shape=outs, in_specs=[hbm] * 5, out_specs=(hbm...]
where the time goes in v5:
time: 80.7 us; the launch traced here: 80.4 us
  Pallas kernels  79.8 us (99%)
    pallas_call x1, Pallas kernels, per_device(): pl.pallas_call(kernel, out_shape=outs, in_specs=[hbm] * 5, out_specs=(hbm...  77.5 us
    pallas_call x1, Pallas kernels, per_device(): pl.pallas_call(place, out_shape=outs, in_specs=[hbm] * 4, out_specs=(hbm,...  2.27 us

profile of v5, /device:TPU:1, one launch (start us, length us, event | category | flops | bytes accessed | tf_op | source)
XLA Modules:
  0.0 80.4 jit_solution(1590791492635592978)
XLA Ops:
  0.6 77.5 %shard_map.84 = (bf16[8,1024]{1,0:T(8,128)(2,1)}, bf16[1024,256]{1,0:T(8,128)(2,1)}, bf16[1024,256]{1,0:T(8,128)(2,1)}, bf16[256,1024]{1,0:T(8,128)(2,1)}) custom-call(bf16[8,1024]{1,0:T(8,128)(2,1)} %tok_hbm.1, bf16[8,1024]{1,0:T(8,128)(2,1)} %grad_hbm.1, bf16[1024,256]{1,0:T(8,128)(2,1)} %gw_hbm.1, bf16[1024,256]{1,0:T(8,128)(2,1)} %uw_hbm.1, ...), custom_call_target="tpu_custom_call" | custom-call | flops 2147483648 | bytes 4194304 | tf_op jit(solution)/shard_map/pallas_call | solution.py:283
  78.1 2.3 %shard_map.85 = (bf16[8,1024]{1,0:T(8,128)(2,1)}, bf16[1024,256]{1,0:T(8,128)(2,1)}, bf16[1024,256]{1,0:T(8,128)(2,1)}, bf16[256,1024]{1,0:T(8,128)(2,1)}) custom-call(bf16[8,1024]{1,0:T(8,128)(2,1)} %get-tuple-element.8.refs_0_, bf16[1024,256]{1,0:T(8,128)(2,1)} %get-tuple-element.9.refs_1_, bf16[1024,256]{1,0:T(8,128)(2,1)} %get-tuple-element.10.refs_2_, ...), custom_call_target="tpu_custom_call" | custom-call | tf_op jit(solution)/shard_map/pallas_call | solution.py:325

commit v6 on v5

--- a/solution.py
+++ b/solution.py
@@ -19,7 +19,7 @@
 
 def kernel(tok_hbm, grad_hbm, gw_hbm, uw_hbm, dw_hbm,
            ig_hbm, gg_hbm, ug_hbm, dg_hbm,
-           tok_ref, grad_ref, gw, uw, dw, ex_out, ex_in, x, part, part_low, gate_part, gate_in, b_in, h, hidden,
+           tok_ref, grad_ref, gw, uw, dw, ex_out, ex_in, x, part, part_low, b_in, h, hidden,
            ig, core_in,
            near_out, near_own, near_in, far_out, far_in,
            ig_ref, gg_ref, ug_ref, dg_ref,
@@ -114,27 +114,22 @@
 
     def products(k):
         rows = x[0, k].reshape(256, 1024)
-        up = dot(rows, uw[...], ((1,), (0,))).reshape(8, 32, 256)
-        hgrad = dot(x[1, k].reshape(256, 1024), dw[...], ((1,), (1,))).reshape(8, 32, 256)
-        part_low[k, :, :, 0:256] = up.astype(BF16)
-        part_low[k, :, :, 256:512] = hgrad.astype(BF16)
-        part[k, :, :, 0:256] = up
-        part[k, :, :, 256:512] = hgrad
-        sums = [push(part_low.at[k, across(dy, dx)], b_in.at[k, s], (gx, across(dy, dx)))
+        for j, v in enumerate((
+                dot(rows, gw[...], ((1,), (0,))), dot(rows, uw[...], ((1,), (0,))),
+                dot(x[1, k].reshape(256, 1024), dw[...], ((1,), (1,))))):
+            v = v.reshape(8, 32, 256)
+            part[k, :, :, 256 * j:256 * j + 256] = v
+            part_low[k, :, :, 256 * j:256 * j + 256] = v.astype(BF16)
+        return [push(part_low.at[k, across(dy, dx)], b_in.at[k, s], (gx, across(dy, dx)))
                 for s, (dy, dx) in enumerate(peers)]
-        gate = dot(rows, gw[...], ((1,), (0,))).reshape(8, 32, 256)
-        gate_part[k] = gate
-        return sums + [push(gate_part.at[k, across(dy, dx)], gate_in.at[k, s], (gx, across(dy, dx)))
-                       for s, (dy, dx) in enumerate(peers)]
 
     def pointwise(k, arrived):
         for cp in arrived:
             cp.wait_recv()
-        total, gate = part[k, gy], gate_part[k, gy]
+        total = part[k, gy]
         for s in range(7):
             total = total + b_in[k, s].astype(F32)
-            gate = gate + gate_in[k, s]
-        up, hgrad = total[:, 0:256], total[:, 256:512]
+        gate, up, hgrad = total[:, 0:256], total[:, 256:512], total[:, 512:768]
         sigma = jax.nn.sigmoid(gate)
         act = gate * sigma
         h[k, gy, :, 0:256] = (hgrad * up * sigma * (1.0 + gate * (1.0 - sigma))).astype(BF16)
@@ -153,25 +148,30 @@
             cols = slice(512 * j, 512 * j + 512)
             v = dot(hh[:, 0:256], gw[cols, :], ((1,), (1,)))
             v = v + dot(hh[:, 256:512], uw[cols, :], ((1,), (1,)))
-            ig[k, :, :, :, cols] = v.reshape(16, 2, 8, 512)
-        return push(ig.at[k, :, 1 - c], core_in.at[k], sibling)
+            ig[k, :, :, :, :, cols] = v.reshape(4, 4, 2, 8, 512)
+        return [push(ig.at[k, :, fs, 1 - c], core_in.at[k, :, fs], sibling)
+                for fs in (pl.ds(2, 1), pl.ds(0, 2), pl.ds(3, 1))]
 
     def send_near(k, arrived):
-        arrived.wait_recv()
-        for n in range(4):
-            for f in range(4):
-                s = 4 * n + f
-                v = ig[k, s, c] + core_in[k, s]
-                v = jnp.concatenate([v[:, 0:512], v[:, 512:1024]], axis=0)
-                if n == 0:
-                    near_own[k, f] = v
-                else:
-                    near_out[k, n, f if n == 3 else PLACE[f]] = v.astype(BF16)
+        def terms(*fs):
+            for n in range(4):
+                for f in fs:
+                    v = ig[k, n, f, c] + core_in[k, n, f]
+                    v = jnp.concatenate([v[:, 0:512], v[:, 512:1024]], axis=0)
+                    if n == 0:
+                        near_own[k, f] = v
+                    else:
+                        near_out[k, n, f if n == 3 else PLACE[f]] = v.astype(BF16)
 
         def to(n, fs, dz):
             return push(near_out.at[k, n, fs], near_in.at[k, n, fs], along(dz))
 
+        arrived[0].wait_recv()
+        terms(2)
         early = [to(n, pl.ds(0, 1), NEAR[n]) for n in (1, 2)]
+        for cp in arrived[1:]:
+            cp.wait_recv()
+        terms(0, 1, 3)
         late = [to(3, pl.ds(0, 2), 2), to(3, pl.ds(2, 2), -2)]
         return early, late + [to(n, pl.ds(1, 3), NEAR[n]) for n in (1, 2)]
 
@@ -294,15 +294,13 @@
             pltpu.VMEM((8, 1024), F32),
             pltpu.VMEM((8, 1024), F32),
             pltpu.VMEM((2, 2, 4, 4, 16, 1024), BF16),
-            pltpu.VMEM((2, 8, 32, 512), F32),
-            pltpu.VMEM((2, 8, 32, 512), BF16),
-            pltpu.VMEM((2, 8, 32, 256), F32),
-            pltpu.VMEM((2, 7, 32, 256), F32),
-            pltpu.VMEM((2, 7, 32, 512), BF16),
+            pltpu.VMEM((2, 8, 32, 768), F32),
+            pltpu.VMEM((2, 8, 32, 768), BF16),
+            pltpu.VMEM((2, 7, 32, 768), BF16),
             pltpu.VMEM((2, 8, 32, 512), BF16),
             pltpu.VMEM((2, 8, 32, 256), BF16),
-            pltpu.VMEM((2, 16, 2, 8, 1024), F32),
-            pltpu.VMEM((2, 16, 8, 1024), F32),
+            pltpu.VMEM((2, 4, 4, 2, 8, 1024), F32),
+            pltpu.VMEM((2, 4, 4, 8, 1024), F32),
             pltpu.VMEM((2, 4, 4, 16, 512), BF16),
             pltpu.VMEM((2, 4, 16, 512), F32),
             pltpu.VMEM((2, 4, 4, 16, 512), BF16),

time: 80.7 us -> 78.9 us (0.978)
  Pallas kernels: 79.8 us -> 77.6 us
    pallas_call x1, Pallas kernels: 77.5 us -> 75.4 us  [per_device(): pl.pallas_call(kernel, out_shape=outs, in_specs=[hbm] * 5, out_specs=(hbm...]
where the time goes in v6:
time: 78.9 us; the launch traced here: 78.3 us
  Pallas kernels  77.6 us (98%)
    pallas_call x1, Pallas kernels, per_device(): pl.pallas_call(kernel, out_shape=outs, in_specs=[hbm] * 5, out_specs=(hbm...  75.4 us
    pallas_call x1, Pallas kernels, per_device(): pl.pallas_call(place, out_shape=outs, in_specs=[hbm] * 4, out_specs=(hbm,...  2.27 us

profile of v6, /device:TPU:1, one launch (start us, length us, event | category | flops | bytes accessed | tf_op | source)
XLA Modules:
  0.0 78.3 jit_solution(13450540670796993082)
XLA Ops:
  0.6 75.4 %shard_map.84 = (bf16[8,1024]{1,0:T(8,128)(2,1)}, bf16[1024,256]{1,0:T(8,128)(2,1)}, bf16[1024,256]{1,0:T(8,128)(2,1)}, bf16[256,1024]{1,0:T(8,128)(2,1)}) custom-call(bf16[8,1024]{1,0:T(8,128)(2,1)} %tok_hbm.1, bf16[8,1024]{1,0:T(8,128)(2,1)} %grad_hbm.1, bf16[1024,256]{1,0:T(8,128)(2,1)} %gw_hbm.1, bf16[1024,256]{1,0:T(8,128)(2,1)} %uw_hbm.1, ...), custom_call_target="tpu_custom_call" | custom-call | flops 2147483648 | bytes 4194304 | tf_op jit(solution)/shard_map/pallas_call | solution.py:283
  76.0 2.3 %shard_map.85 = (bf16[8,1024]{1,0:T(8,128)(2,1)}, bf16[1024,256]{1,0:T(8,128)(2,1)}, bf16[1024,256]{1,0:T(8,128)(2,1)}, bf16[256,1024]{1,0:T(8,128)(2,1)}) custom-call(bf16[8,1024]{1,0:T(8,128)(2,1)} %get-tuple-element.8.refs_0_, bf16[1024,256]{1,0:T(8,128)(2,1)} %get-tuple-element.9.refs_1_, bf16[1024,256]{1,0:T(8,128)(2,1)} %get-tuple-element.10.refs_2_, ...), custom_call_target="tpu_custom_call" | custom-call | tf_op jit(solution)/shard_map/pallas_call | solution.py:323

commit v7 on v6

--- a/solution.py
+++ b/solution.py
@@ -46,7 +46,7 @@
 
     barrier = pltpu.get_barrier_semaphore()
     met = [along(dz) for dz in (8, 4, -4, 2, -2, 1, -1)]
-    met += [along(dz, other_x=True) for dz in (8, 4, -4, 0)]
+    met += [along(dz, other_x=True) for dz in (8, 4, -4, 1, -1, 0)]
     met += [along(other_core=True)]
     met += [(gx, across(dy, dx)) for dy, dx in peers]
     for dev in met:
@@ -80,11 +80,11 @@
         [jnp.where(first, mine, theirs), jnp.where(first, theirs, mine)], axis=0)
     x[c, 0, 0, 0] = block.astype(BF16)
 
-    shared, arriving = [], {}
+    shared, arriving, crossed = [], {}, {}
 
     def share(n, f):
         ours = x.at[c, 0, n, f]
-        from_x = push(ours, x.at[c, 1, n, f], partner)
+        from_x = crossed.get((n, f)) or push(ours, x.at[c, 1, n, f], partner)
         shared.append((push(ours, ours, sibling), from_x, n, f))
 
     def to_near(f):
@@ -95,6 +95,9 @@
             arriving[3, (f + 3) % 4] = push(ours, x.at[c, 0, 3, (f + 3) % 4], along(2))
         for n in (1, 2):
             arriving[n, f] = push(ours, x.at[c, 0, n, f], along(-NEAR[n]))
+        if f == 2:
+            for n in (1, 2):
+                crossed[n, f] = push(ours, x.at[c, 1, n, f], along(-NEAR[n], other_x=True))
 
     def pass_on(*slots):
         for slot in slots:
@@ -217,10 +220,9 @@
     c1 = pointwise(1, b1)
     i0 = input_products(0, c0)
     n0 = send_near(0, i0)
-    spread_hidden = spread(0, hidden)
     i1 = input_products(1, c1)
     n1 = send_near(1, i1)
-    spread_hidden += spread(1, hidden)
+    spread_hidden = spread(0, hidden) + spread(1, hidden)
     f0 = send_far(0, *n0)
     f1 = send_far(1, *n1)
 
@@ -262,10 +264,15 @@
 
 def place(*refs):
     given, wanted, held, load_sem, store_sem = refs[:4], refs[4:8], refs[8:12], refs[12], refs[13]
-    loads = [pltpu.make_async_copy(s, v, load_sem.at[i])
-             for i, (s, v) in enumerate(zip(given, held))]
-    stores = [pltpu.make_async_copy(v, d, store_sem.at[i])
-              for i, (v, d) in enumerate(zip(held, wanted))]
+    loads, stores = [], []
+    for s, v, d in zip(given, held, wanted):
+        parts = 1 if s.shape[0] == 8 else 4
+        rows = s.shape[0] // parts
+        for i in range(parts):
+            cut = pl.ds(i * rows, rows)
+            k = len(loads)
+            loads.append(pltpu.make_async_copy(s.at[cut], v.at[cut], load_sem.at[k]))
+            stores.append(pltpu.make_async_copy(v.at[cut], d.at[cut], store_sem.at[k]))
     for cp in loads:
         cp.start()
     for load, store in zip(loads, stores):
@@ -326,7 +333,7 @@
         in_specs=[hbm] * 4,
         out_specs=(hbm,) * 4,
         scratch_shapes=[pltpu.VMEM(o.shape, BF16) for o in outs]
-        + [pltpu.SemaphoreType.DMA((4,))] * 2,
+        + [pltpu.SemaphoreType.DMA((13,))] * 2,
         compiler_params=pltpu.CompilerParams(vmem_limit_bytes=60 << 20),
     )(*results)
 

time: 78.9 us -> 78.4 us (level)
  no operation moved by 1% of the time
where the time goes in v7:
time: 78.4 us; the launch traced here: 78.1 us
  Pallas kernels  77.5 us (99%)
    pallas_call x1, Pallas kernels, per_device(): pl.pallas_call(kernel, out_shape=outs, in_specs=[hbm] * 5, out_specs=(hbm...  75.1 us
    pallas_call x1, Pallas kernels, per_device(): pl.pallas_call(place, out_shape=outs, in_specs=[hbm] * 4, out_specs=(hbm,...  2.36 us

profile of v7, /device:TPU:1, one launch (start us, length us, event | category | flops | bytes accessed | tf_op | source)
XLA Modules:
  0.0 78.1 jit_solution(638578927207297136)
XLA Ops:
  0.6 75.1 %shard_map.84 = (bf16[8,1024]{1,0:T(8,128)(2,1)}, bf16[1024,256]{1,0:T(8,128)(2,1)}, bf16[1024,256]{1,0:T(8,128)(2,1)}, bf16[256,1024]{1,0:T(8,128)(2,1)}) custom-call(bf16[8,1024]{1,0:T(8,128)(2,1)} %tok_hbm.1, bf16[8,1024]{1,0:T(8,128)(2,1)} %grad_hbm.1, bf16[1024,256]{1,0:T(8,128)(2,1)} %gw_hbm.1, bf16[1024,256]{1,0:T(8,128)(2,1)} %uw_hbm.1, ...), custom_call_target="tpu_custom_call" | custom-call | flops 2147483648 | bytes 4194304 | tf_op jit(solution)/shard_map/pallas_call | solution.py:290
  75.7 2.4 %shard_map.85 = (bf16[8,1024]{1,0:T(8,128)(2,1)}, bf16[1024,256]{1,0:T(8,128)(2,1)}, bf16[1024,256]{1,0:T(8,128)(2,1)}, bf16[256,1024]{1,0:T(8,128)(2,1)}) custom-call(bf16[8,1024]{1,0:T(8,128)(2,1)} %get-tuple-element.8.refs_0_, bf16[1024,256]{1,0:T(8,128)(2,1)} %get-tuple-element.9.refs_1_, bf16[1024,256]{1,0:T(8,128)(2,1)} %get-tuple-element.10.refs_2_, ...), custom_call_target="tpu_custom_call" | custom-call | tf_op jit(solution)/shard_map/pallas_call | solution.py:330

commit v8 on v7

--- a/solution.py
+++ b/solution.py
@@ -45,8 +45,8 @@
         cp.start()
 
     barrier = pltpu.get_barrier_semaphore()
-    met = [along(dz) for dz in (8, 4, -4, 2, -2, 1, -1)]
-    met += [along(dz, other_x=True) for dz in (8, 4, -4, 1, -1, 0)]
+    met = [along(dz) for dz in (4, -4, 2, -2, 1, -1)]
+    met += [along(dz, other_x=True) for dz in (4, -4, 1, -1, 0)]
     met += [along(other_core=True)]
     met += [(gx, across(dy, dx)) for dy, dx in peers]
     for dev in met:
@@ -104,15 +104,21 @@
             arriving.pop(slot).wait_recv()
             share(*slot)
 
-    for i in FAR_ORDER:
+    for i in (1, 3):
         arriving[0, 4 - i] = push(x.at[c, 0, 0, 0], x.at[c, 0, 0, 4 - i], along(4 * i))
     to_near(0)
     share(0, 0)
     pass_on((1, 0), (2, 0), (3, 0), (3, 3))
-    for f in (1, 3, 2):
+    halves = []
+    for f, cols, dz in ((1, pl.ds(0, 512), -4), (3, pl.ds(512, 512), 4)):
         arriving.pop((0, f)).wait_recv()
+        halves.append(push(x.at[c, 0, 0, f, :, cols], x.at[c, 0, 0, 2, :, cols], along(dz)))
         to_near(f)
         share(0, f)
+    for cp in halves:
+        cp.wait_recv()
+    to_near(2)
+    share(0, 2)
     pass_on((1, 1), (2, 1), (3, 1), (1, 3), (2, 3), (3, 2), (1, 2), (2, 2))
 
     def products(k):

time: 78.4 us -> 75.7 us (0.966); the launches traced: 78.1 us -> 74.4 us
  Pallas kernels: 77.5 us -> 73.8 us
    pallas_call x1, Pallas kernels: 75.1 us -> 71.4 us  [per_device(): pl.pallas_call(kernel, out_shape=outs, in_specs=[hbm] * 5, out_specs=(hbm...]
where the time goes in v8:
time: 75.7 us; the launch traced here: 74.4 us
  Pallas kernels  73.8 us (97%)
    pallas_call x1, Pallas kernels, per_device(): pl.pallas_call(kernel, out_shape=outs, in_specs=[hbm] * 5, out_specs=(hbm...  71.4 us
    pallas_call x1, Pallas kernels, per_device(): pl.pallas_call(place, out_shape=outs, in_specs=[hbm] * 4, out_specs=(hbm,...  2.36 us

profile of v8, /device:TPU:1, one launch (start us, length us, event | category | flops | bytes accessed | tf_op | source)
XLA Modules:
  0.0 74.4 jit_solution(7347797270660563052)
XLA Ops:
  0.6 71.4 %shard_map.84 = (bf16[8,1024]{1,0:T(8,128)(2,1)}, bf16[1024,256]{1,0:T(8,128)(2,1)}, bf16[1024,256]{1,0:T(8,128)(2,1)}, bf16[256,1024]{1,0:T(8,128)(2,1)}) custom-call(bf16[8,1024]{1,0:T(8,128)(2,1)} %tok_hbm.1, bf16[8,1024]{1,0:T(8,128)(2,1)} %grad_hbm.1, bf16[1024,256]{1,0:T(8,128)(2,1)} %gw_hbm.1, bf16[1024,256]{1,0:T(8,128)(2,1)} %uw_hbm.1, ...), custom_call_target="tpu_custom_call" | custom-call | flops 2147483648 | bytes 4194304 | tf_op jit(solution)/shard_map/pallas_call | solution.py:296
  72.1 2.4 %shard_map.85 = (bf16[8,1024]{1,0:T(8,128)(2,1)}, bf16[1024,256]{1,0:T(8,128)(2,1)}, bf16[1024,256]{1,0:T(8,128)(2,1)}, bf16[256,1024]{1,0:T(8,128)(2,1)}) custom-call(bf16[8,1024]{1,0:T(8,128)(2,1)} %get-tuple-element.8.refs_0_, bf16[1024,256]{1,0:T(8,128)(2,1)} %get-tuple-element.9.refs_1_, bf16[1024,256]{1,0:T(8,128)(2,1)} %get-tuple-element.10.refs_2_, ...), custom_call_target="tpu_custom_call" | custom-call | tf_op jit(solution)/shard_map/pallas_call | solution.py:336

commit v9 on v8

--- a/solution.py
+++ b/solution.py
@@ -46,7 +46,7 @@
 
     barrier = pltpu.get_barrier_semaphore()
     met = [along(dz) for dz in (4, -4, 2, -2, 1, -1)]
-    met += [along(dz, other_x=True) for dz in (4, -4, 1, -1, 0)]
+    met += [along(dz, other_x=True) for dz in (1, -1, 0)]
     met += [along(other_core=True)]
     met += [(gx, across(dy, dx)) for dy, dx in peers]
     for dev in met:

time: 75.7 us -> 75.3 us (level)
  no operation moved by 1% of the time
where the time goes in v9:
time: 75.3 us; the launch traced here: 74 us
  Pallas kernels  73.4 us (97%)
    pallas_call x1, Pallas kernels, per_device(): pl.pallas_call(kernel, out_shape=outs, in_specs=[hbm] * 5, out_specs=(hbm...  71 us
    pallas_call x1, Pallas kernels, per_device(): pl.pallas_call(place, out_shape=outs, in_specs=[hbm] * 4, out_specs=(hbm,...  2.36 us

profile of v9, /device:TPU:1, one launch (start us, length us, event | category | flops | bytes accessed | tf_op | source)
XLA Modules:
  0.0 74.0 jit_solution(3909948556746113117)
XLA Ops:
  0.6 71.0 %shard_map.84 = (bf16[8,1024]{1,0:T(8,128)(2,1)}, bf16[1024,256]{1,0:T(8,128)(2,1)}, bf16[1024,256]{1,0:T(8,128)(2,1)}, bf16[256,1024]{1,0:T(8,128)(2,1)}) custom-call(bf16[8,1024]{1,0:T(8,128)(2,1)} %tok_hbm.1, bf16[8,1024]{1,0:T(8,128)(2,1)} %grad_hbm.1, bf16[1024,256]{1,0:T(8,128)(2,1)} %gw_hbm.1, bf16[1024,256]{1,0:T(8,128)(2,1)} %uw_hbm.1, ...), custom_call_target="tpu_custom_call" | custom-call | flops 2147483648 | bytes 4194304 | tf_op jit(solution)/shard_map/pallas_call | solution.py:296
  71.6 2.4 %shard_map.85 = (bf16[8,1024]{1,0:T(8,128)(2,1)}, bf16[1024,256]{1,0:T(8,128)(2,1)}, bf16[1024,256]{1,0:T(8,128)(2,1)}, bf16[256,1024]{1,0:T(8,128)(2,1)}) custom-call(bf16[8,1024]{1,0:T(8,128)(2,1)} %get-tuple-element.8.refs_0_, bf16[1024,256]{1,0:T(8,128)(2,1)} %get-tuple-element.9.refs_1_, bf16[1024,256]{1,0:T(8,128)(2,1)} %get-tuple-element.10.refs_2_, ...), custom_call_target="tpu_custom_call" | custom-call | tf_op jit(solution)/shard_map/pallas_call | solution.py:336

commit v10 on v9

--- a/solution.py
+++ b/solution.py
@@ -113,6 +113,7 @@
     for f, cols, dz in ((1, pl.ds(0, 512), -4), (3, pl.ds(512, 512), 4)):
         arriving.pop((0, f)).wait_recv()
         halves.append(push(x.at[c, 0, 0, f, :, cols], x.at[c, 0, 0, 2, :, cols], along(dz)))
+    for f in (1, 3):
         to_near(f)
         share(0, f)
     for cp in halves:
@@ -218,11 +219,11 @@
         from_x.wait_recv()
         other = x.at[c, 1, n, f]
         to_core.append(push(other, other, sibling))
+    c0 = pointwise(0, b0)
     for cp in to_core:
         cp.wait_recv()
     b1 = products(1)
 
-    c0 = pointwise(0, b0)
     c1 = pointwise(1, b1)
     i0 = input_products(0, c0)
     n0 = send_near(0, i0)

time: 75.3 us -> 78 us (1.036); the launches traced: 74 us -> 77.7 us
  Pallas kernels: 73.4 us -> 77 us
    pallas_call x1, Pallas kernels: 71 us -> 74.7 us  [per_device(): pl.pallas_call(kernel, out_shape=outs, in_specs=[hbm] * 5, out_specs=(hbm...]
where the time goes in v10:
time: 78 us; the launch traced here: 77.7 us
  Pallas kernels  77 us (99%)
    pallas_call x1, Pallas kernels, per_device(): pl.pallas_call(kernel, out_shape=outs, in_specs=[hbm] * 5, out_specs=(hbm...  74.7 us
    pallas_call x1, Pallas kernels, per_device(): pl.pallas_call(place, out_shape=outs, in_specs=[hbm] * 4, out_specs=(hbm,...  2.36 us

profile of v10, /device:TPU:1, one launch (start us, length us, event | category | flops | bytes accessed | tf_op | source)
XLA Modules:
  0.0 77.7 jit_solution(11509473037042111042)
XLA Ops:
  0.6 74.7 %shard_map.84 = (bf16[8,1024]{1,0:T(8,128)(2,1)}, bf16[1024,256]{1,0:T(8,128)(2,1)}, bf16[1024,256]{1,0:T(8,128)(2,1)}, bf16[256,1024]{1,0:T(8,128)(2,1)}) custom-call(bf16[8,1024]{1,0:T(8,128)(2,1)} %tok_hbm.1, bf16[8,1024]{1,0:T(8,128)(2,1)} %grad_hbm.1, bf16[1024,256]{1,0:T(8,128)(2,1)} %gw_hbm.1, bf16[1024,256]{1,0:T(8,128)(2,1)} %uw_hbm.1, ...), custom_call_target="tpu_custom_call" | custom-call | flops 2147483648 | bytes 4194304 | tf_op jit(solution)/shard_map/pallas_call | solution.py:297
  75.3 2.4 %shard_map.85 = (bf16[8,1024]{1,0:T(8,128)(2,1)}, bf16[1024,256]{1,0:T(8,128)(2,1)}, bf16[1024,256]{1,0:T(8,128)(2,1)}, bf16[256,1024]{1,0:T(8,128)(2,1)}) custom-call(bf16[8,1024]{1,0:T(8,128)(2,1)} %get-tuple-element.8.refs_0_, bf16[1024,256]{1,0:T(8,128)(2,1)} %get-tuple-element.9.refs_1_, bf16[1024,256]{1,0:T(8,128)(2,1)} %get-tuple-element.10.refs_2_, ...), custom_call_target="tpu_custom_call" | custom-call | tf_op jit(solution)/shard_map/pallas_call | solution.py:337
